TPU v7x, 32 devices: a whole 2x2x4 slice. The times are simulated.
32 devices in a mesh: section: 16 (over z, y, x), tp: 2 (over core).
Axes of the slice: x: 2, y: 2, z: 4, core: 2. Of those that a mesh axis runs over, the one named last changes fastest.
Arguments:
- prefill_hidden: bfloat16 [4096, 8192], P('section', 'tp'), may hold values from -180 to 180
- norm_gain: float32 [8192], replicated, may hold values from 0.25 to 1.75
- key_weight: bfloat16 [8192, 1024], P(None, 'tp'), may hold values from -0.0625 to 0.0625
- value_weight: bfloat16 [8192, 1024], P(None, 'tp'), may hold values from -0.0625 to 0.0625
- prefill_query: bfloat16 [4096, 8192], P('section', 'tp'), may hold values from -102 to 102
- resident_keys: bfloat16 [4096, 16, 1024], P('section', None, 'tp'), may hold values from -6 to 6
- resident_values: bfloat16 [4096, 16, 1024], P('section', None, 'tp'), may hold values from -6 to 6
- decode_query: bfloat16 [256, 8192], P('section', 'tp'), may hold values from -102 to 102
- page_owner: int32 [256], P('section'), may hold values from 0 to 15, as said below
- block_table: int32 [256, 62], P('section'), may hold values from 0 to 287, as said below
- context_len: int32 [256], P('section'), may hold values from 1 to 992, as said below
Outputs:
- prefill_attention: bfloat16 [4096, 8192], P('section', 'tp')
- decode_attention: bfloat16 [256, 8192], P('section', 'tp')
Inputs may be any that keep to these rules, and one draw needn't show every extreme that they name: `page_owner`: the 16 pages of each section device go to 8 different owners, exactly 2 pages to each; one owner receives pages from every section device. `block_table`: row entries name first the row's resident pages (below 256), then 256 + page_slot for at most 2 pages sent to the row's owner; every page sent to an owner is named by exactly one of its rows; entries after a row's pages are 0. `context_len`: A row's last visible token lies in the last page its table names.
All inputs are finite; a program needn't handle non-finite values.
Results may differ from a plain program's by a relative error of at most 0.011.
Values may be sent and summed in bfloat16 or wider, within the bound.
No kernel may reach another device: no remote copies, remote signals or barrier semaphores. Data moves between devices by JAX's collectives and lax.ppermute only.
A program may use at most 256 MiB of HBM per device.

v0:
```python
import math

import jax
import jax.numpy as jnp
from jax import lax
from jax.sharding import PartitionSpec as P

HD = 128
PAGE = 16
CAP = 2


NORM_EPSILON = 1e-05
ROPE_THETA = 500000.0
NEG_LARGE = -1e30


def rotate_keys(raw_keys, positions):
    head_width = raw_keys.shape[-1]
    half_width = head_width // 2
    frequency = jnp.exp(
        jnp.arange(half_width, dtype=jnp.float32) * (-2.0 * math.log(ROPE_THETA) / head_width)
    )
    angles = positions.astype(jnp.float32)[:, None] * frequency[None, :]
    cosine = jnp.cos(angles)[:, None, :]
    sine_part = jnp.sin(angles)[:, None, :]
    first_half = raw_keys[..., :half_width]
    second_half = raw_keys[..., half_width:]
    return jnp.concatenate(
        [
            first_half * cosine - second_half * sine_part,
            second_half * cosine + first_half * sine_part,
        ],
        axis=-1,
    )


def empty_state(kv_heads, group_size, query_rows, head_width):
    return (
        jnp.full((kv_heads, group_size, query_rows), NEG_LARGE, jnp.float32),
        jnp.zeros((kv_heads, group_size, query_rows), jnp.float32),
        jnp.zeros((kv_heads, group_size, query_rows, head_width), jnp.float32),
    )


def attend_piece(carried, queries, query_pos, key_piece, value_piece, key_pos, score_scale):
    kv_heads = queries.shape[1]
    head_width = queries.shape[3]

    def compute(current):
        row_max, row_sum, weighted = current
        piece_rows = key_piece.shape[0]
        key_block = key_piece.reshape(piece_rows, kv_heads, head_width)
        value_block = value_piece.reshape(piece_rows, kv_heads, head_width)
        scores = (
            jnp.einsum("tkgd,rkd->kgtr", queries, key_block, preferred_element_type=jnp.float32)
            * score_scale
        )
        visible = key_pos[None, :] <= query_pos[:, None]
        scores = jnp.where(visible, scores, NEG_LARGE)
        new_max = jnp.maximum(row_max, jnp.max(scores, axis=-1))
        weights = jnp.where(visible, jnp.exp(scores - new_max[..., None]), 0.0)
        new_sum = jnp.sum(weights, axis=-1)
        product = jnp.einsum(
            "kgtr,rkd->kgtd",
            weights.astype(jnp.bfloat16),
            value_block,
            preferred_element_type=jnp.float32,
        )
        return (new_max, new_sum, product)

    return lax.cond(
        jnp.min(key_pos) > jnp.max(query_pos), lambda current: current, compute, carried
    )


def finish_state(carried):
    row_max, row_sum, weighted = carried
    result = weighted / row_sum[..., None]
    kv_heads, group_size, query_rows, head_width = result.shape
    return (
        jnp.transpose(result, (2, 0, 1, 3))
        .reshape(query_rows, kv_heads * group_size * head_width)
        .astype(jnp.bfloat16)
    )


def per_device(
    prefill_hidden,
    norm_gain,
    key_weight,
    value_weight,
    prefill_query,
    resident_keys,
    resident_values,
    decode_query,
    page_owner,
    block_table,
    context_len,
):
    section_count = lax.axis_size("section")
    section_index = lax.axis_index("section")
    stretch_rows = prefill_hidden.shape[0]
    key_width = key_weight.shape[1]
    head_width = HD
    kv_heads = key_width // head_width
    query_width = prefill_query.shape[1]
    group_size = query_width // key_width
    score_scale = 1.0 / math.sqrt(head_width)
    features = lax.all_gather(prefill_hidden, "tp", axis=1, tiled=True)
    feature_f32 = features.astype(jnp.float32)
    inverse_rms = lax.rsqrt(
        jnp.mean(feature_f32 * feature_f32, axis=1, keepdims=True) + NORM_EPSILON
    )
    normed = (feature_f32 * inverse_rms * norm_gain).astype(jnp.bfloat16)
    raw_keys = jnp.dot(normed, key_weight, preferred_element_type=jnp.float32)
    value_rows = jnp.dot(normed, value_weight, preferred_element_type=jnp.float32).astype(
        jnp.bfloat16
    )
    positions = section_index * stretch_rows + jnp.arange(stretch_rows, dtype=jnp.int32)
    key_rows = (
        rotate_keys(raw_keys.reshape(stretch_rows, kv_heads, head_width), positions)
        .reshape(stretch_rows, key_width)
        .astype(jnp.bfloat16)
    )
    queries = prefill_query.reshape(stretch_rows, kv_heads, group_size, head_width)
    pieces = (
        lax.all_gather(key_rows, "section", axis=0, tiled=True),
        lax.all_gather(value_rows, "section", axis=0, tiled=True),
    )
    key_pos = jnp.arange(pieces[0].shape[0], dtype=jnp.int32)
    folded = attend_piece(
        empty_state(kv_heads, group_size, stretch_rows, head_width),
        queries,
        positions,
        pieces[0],
        pieces[1],
        key_pos,
        score_scale,
    )
    prefill_attention = finish_state(folded)
    pages_here = stretch_rows // PAGE
    page_data = jnp.concatenate([key_rows, value_rows], axis=1).reshape(
        pages_here, PAGE * 2 * key_width
    )
    page_index = jnp.arange(pages_here, dtype=jnp.int32)
    same_owner = (page_owner[:, None] == page_owner[None, :]) & (
        page_index[None, :] < page_index[:, None]
    )
    page_rank = jnp.sum(same_owner.astype(jnp.int32), axis=1)
    slot_index = page_owner * CAP + page_rank
    placement_matrix = (
        jnp.arange(section_count * CAP, dtype=jnp.int32)[:, None] == slot_index[None, :]
    ).astype(jnp.bfloat16)
    outgoing = jnp.dot(placement_matrix, page_data, preferred_element_type=jnp.float32).astype(
        jnp.bfloat16
    )
    outgoing = outgoing.reshape(section_count, CAP, PAGE * 2 * key_width)
    arrived = lax.all_to_all(outgoing, "section", split_axis=0, concat_axis=0, tiled=True).reshape(
        section_count * CAP, PAGE, 2 * key_width
    )
    cache_keys = jnp.concatenate([resident_keys, arrived[:, :, :key_width]], axis=0)
    cache_values = jnp.concatenate([resident_values, arrived[:, :, key_width:]], axis=0)
    decode_rows = decode_query.shape[0]
    key_span = block_table.shape[1] * PAGE
    gathered_keys = cache_keys[block_table].reshape(decode_rows, key_span, kv_heads, head_width)
    gathered_values = cache_values[block_table].reshape(decode_rows, key_span, kv_heads, head_width)
    decode_queries = decode_query.reshape(decode_rows, kv_heads, group_size, head_width)
    scores = (
        jnp.einsum(
            "bkgd,blkd->bkgl", decode_queries, gathered_keys, preferred_element_type=jnp.float32
        )
        * score_scale
    )
    visible = (jnp.arange(key_span, dtype=jnp.int32)[None, :] < context_len[:, None])[
        :, None, None, :
    ]
    scores = jnp.where(visible, scores, NEG_LARGE)
    row_max = jnp.max(scores, axis=-1, keepdims=True)
    weights = jnp.exp(scores - row_max)
    row_sum = jnp.sum(weights, axis=-1, keepdims=True)
    attended = (
        jnp.einsum(
            "bkgl,blkd->bkgd",
            weights.astype(jnp.bfloat16),
            gathered_values,
            preferred_element_type=jnp.float32,
        )
        / row_sum
    )
    decode_attention = attended.reshape(decode_rows, query_width).astype(jnp.bfloat16)
    return (prefill_attention, decode_attention)


def solution(mesh):
    return jax.shard_map(
        per_device,
        mesh=mesh,
        in_specs=(
            P("section", "tp"),
            P(),
            P(None, "tp"),
            P(None, "tp"),
            P("section", "tp"),
            P("section", None, "tp"),
            P("section", None, "tp"),
            P("section", "tp"),
            P("section"),
            P("section", None),
            P("section"),
        ),
        out_specs=(P("section", "tp"), P("section", "tp")),
        check_vma=False,
    )
```

profile of v0, /device:TPU:0, one launch (start us, length us, event | category | flops | bytes accessed | tf_op | source)
XLA Modules:
  0.0 380.4 jit_solution(883591309371658387)
XLA Ops:
  7.2 0.0 all-gather.4.cloned.1.call-start
  7.2 0.7 all-gather.4.cloned.1.call-update
  7.9 0.0 all-gather.6.cloned.1.call-start
  8.0 0.6 fusion.40
  8.6 0.5 multiply_cosine_fusion
  9.1 16.8 %all-gather.4.cloned.1.call-done = bf16[256,8192]{1,0:T(8,128)(2,1)} async-done(((bf16[256,4096]{1,0:T(8,128)(2,1)}), bf16[256,8192]{1,0:T(8,128)(2,1)}) %all-gather.4.cloned.1.call-update) | async-done | bytes 4194320 | tf_op jit(solution)/shard_map/all_gather | solution.py:110
  26.0 3.1 fusion.17
  29.1 7.0 %fusion.25 = f32[256,512]{1,0:T(8,128)S(1)} fusion(bf16[8192,512]{1,0:T(8,128)(2,1)} %param.15, bf16[256,8192]{1,0:T(8,128)(2,1)} %all-gather.4.cloned.1.call-done, f32[8192]{0:T(1024)S(1)} %copy-done.5, f32[256]{0:T(256)S(1)} %add_rsqrt_fusion), kind=kOutput, calls=%fused_computation.40 | convolution fusion | flops 2155872256 | bytes 13140992 | tf_op jit(solution)/shard_map/dot_general | solution.py:116
  36.1 0.2 reshape.135
  36.3 0.5 subtract_convert_fusion
  36.8 0.4 pad_maximum_fusion.3
  37.2 0.7 copy.64
  37.9 0.0 all-gather.6.cloned.1.call-update
  38.0 0.0 all-gather.8.cloned.1.call-start
  38.0 7.8 %convolution_convert_fusion.1 = bf16[256,512]{1,0:T(8,128)(2,1)} fusion(bf16[8192,512]{1,0:T(8,128)(2,1)} %param.16, bf16[256,8192]{1,0:T(8,128)(2,1)} %all-gather.4.cloned.1.call-done, f32[8192]{0:T(1024)S(1)} %copy-done.5, f32[256]{0:T(256)S(1)} %add_rsqrt_fusion), kind=kOutput, calls=%fused_computation.39 | convolution fusion | flops 2156003328 | bytes 12878848 | tf_op jit(solution)/shard_map/dot_general | solution.py:117
  45.8 0.2 convert_reduce_fusion
  46.0 1.0 pad_maximum_fusion.2
  47.0 0.2 reshape.136
  47.3 0.4 convolution_convert_fusion
  47.7 1.5 reshape.137
  49.2 6.8 %all-to-all-start = ((bf16[16,2,16384]{2,1,0:T(2,128)(2,1)}), bf16[16,2,16384]{2,1,0:T(2,128)(2,1)S(1)}, u32[]{:S(2)}, u32[]{:S(2)}) async-start(bf16[16,2,16384]{2,1,0:T(2,128)(2,1)} %reshape.137), calls=%async_computation | async-start | bytes 2097152 | tf_op jit(solution)/shard_map/all_to_all | solution.py:159
  56.0 0.1 reshape.144
  56.8 0.1 iota_compare_fusion
  56.9 30.9 %all-to-all-done = bf16[16,2,16384]{2,1,0:T(2,128)(2,1)S(1)} async-done(((bf16[16,2,16384]{2,1,0:T(2,128)(2,1)}), bf16[16,2,16384]{2,1,0:T(2,128)(2,1)S(1)}, u32[]{:S(2)}, u32[]{:S(2)}) %all-to-all-start) | async-done | bytes 1048608 | tf_op jit(solution)/shard_map/all_to_all | solution.py:159
  87.8 0.8 reshape.138
  88.7 0.1 fusion.44
  88.8 4.7 %pad_maximum_fusion = bf16[288,16,512]{2,1,0:T(8,128)(2,1)} fusion(bf16[32,16,512]{2,1,0:T(8,128)(2,1)S(1)} %get-tuple-element.26, bf16[256,16,512]{2,1,0:T(8,128)(2,1)} %param.18), kind=kLoop, calls=%fused_computation.28 | loop fusion | flops 2359296 | bytes 9437184 | tf_op jit(solution)/shard_map/concatenate | solution.py:162
  93.5 14.6 %gather_fusion = bf16[992,16,512]{2,1,0:T(8,128)(2,1)} fusion(bf16[288,16,512]{2,1,0:T(8,128)(2,1)} %pad_maximum_fusion, s32[1024]{0:T(1024)S(1)} %pad_clamp_fusion), kind=kCustom, calls=%fused_computation | custom fusion | bytes 32509824 | tf_op jit(solution)/shard_map/gather | solution.py:166
  108.2 23.1 %reshape.139 = bf16[16,992,4,128]{3,2,1,0:T(4,128)(2,1)} reshape(bf16[992,16,512]{2,1,0:T(8,128)(2,1)} %gather_fusion) | data formatting | bytes 32505856 | tf_op jit(solution)/shard_map/reshape | solution.py:166
  131.3 4.8 %pad_maximum_fusion.1 = bf16[288,16,512]{2,1,0:T(8,128)(2,1)} fusion(bf16[32,16,512]{2,1,0:T(8,128)(2,1)S(1)} %get-tuple-element.27, bf16[256,16,512]{2,1,0:T(8,128)(2,1)} %param.19), kind=kLoop, calls=%fused_computation.29 | loop fusion | flops 2359296 | bytes 9437184 | tf_op jit(solution)/shard_map/concatenate | solution.py:163
  136.1 14.8 %gather_fusion.1 = bf16[992,16,512]{2,1,0:T(8,128)(2,1)} fusion(bf16[288,16,512]{2,1,0:T(8,128)(2,1)} %pad_maximum_fusion.1, s32[1024]{0:T(1024)S(1)} %pad_clamp_fusion), kind=kCustom, calls=%fused_computation.1 | custom fusion | bytes 32509824 | tf_op jit(solution)/shard_map/gather | solution.py:167
  150.9 23.0 %reshape.141 = bf16[16,992,4,128]{3,2,1,0:T(4,128)(2,1)} reshape(bf16[992,16,512]{2,1,0:T(8,128)(2,1)} %gather_fusion.1) | data formatting | bytes 32505856 | tf_op jit(solution)/shard_map/reshape | solution.py:167
  173.9 9.0 %bitcast_reduce_fusion = (f32[16,4,8]{2,1,0:T(4,128)S(1)}, f32[16,4,992,8]{2,3,1,0:T(8,128)S(1)}) fusion(pred[16,992]{1,0:T(8,128)(4,1)S(1)} %iota_compare_fusion, bf16[16,4,8,128]{3,2,1,0:T(8,128)(2,1)S(1)} %bitcast.60, bf16[16,992,4,128]{3,2,1,0:T(4,128)(2,1)} %reshape.139), kind=kOutput, calls=%fused_computation.33 | convolution fusion | flops 131546624 | bytes 18433536 | tf_op jit(solution)/shard_map/bkgd,blkd->bkgl/dot_general | solution.py:170
  182.9 0.7 fusion.22
  183.6 8.4 %fusion.30 = bf16[16,4,8,128]{3,2,1,0:T(8,128)(2,1)S(1)} fusion(bf16[16,992,4,128]{3,2,1,0:T(4,128)(2,1)} %reshape.141, f32[16,4,992,8]{2,3,1,0:T(8,128)S(1)} %get-tuple-element.33, f32[16,4,8]{2,1,0:T(4,128)S(1)} %get-tuple-element.32, pred[16,992]{1,0:T(8,128)(4,1)S(1)} %iota_compare_fusion, f32[16,4,8]{2,1,0:T(4,128)S(1)} %fusion.22), kind=kOutput, calls=%fused_computation.42 | convolution fusion | flops 132186112 | bytes 18435584 | tf_op jit(solution)/shard_map/bkgl,blkd->bkgd/dot_general | solution.py:183
  192.0 0.7 copy.65
  192.7 13.0 %all-gather.8.cloned.1.call-done = bf16[4096,512]{1,0:T(8,128)(2,1)} async-done(((bf16[256,512]{1,0:T(8,128)(2,1)}), bf16[4096,512]{1,0:T(8,128)(2,1)}) %all-gather.8.cloned.1.call-update) | async-done | bytes 4194320 | tf_op jit(solution)/shard_map/all_gather | solution.py:129
  205.8 161.5 %conditional.1 = (f32[4,8,256]{2,1,0:T(8,128)S(1)}, f32[4,8,256,128]{3,2,1,0:T(8,128)}) conditional(s32[]{:T(128)} %convert_element_type.51, (s32[4096]{0:T(1024)S(1)}, s32[256]{0:T(256)S(1)}, bf16[4096,512]{1,0:T(8,128)(2,1)}, bf16[256,4096]{1,0:T(8,128)(2,1)S(1)}, bf16[4096,512]{1,0:T(8,128)(2,1)}) %tuple.33, () %tuple.17), branch_computations={%region_2.5_spmd, %region_5.0_spmd} | conditional | flops 17617117184 | bytes 442713088 | solution.py:72
  205.8 1.9 broadcast_compare_fusion
  207.6 6.9 %reshape.125 = bf16[4096,4,128]{2,1,0:T(4,128)(2,1)} reshape(bf16[4096,512]{1,0:T(8,128)(2,1)} %get-tuple-element.13) | data formatting | bytes 8388608 | tf_op jit(solution)/shard_map/cond/branch_0_fun/reshape | solution.py:53
  214.5 1.8 copy.35
  216.4 48.2 %fusion = (f32[4,8,256]{2,1,0:T(8,128)S(1)}, f32[4,4096,256,8]{2,1,3,0:T(8,128)}) fusion(pred[256,4096]{0,1:T(8,128)(4,1)S(1)} %broadcast_compare_fusion, bf16[256,4,8,128]{3,2,1,0:T(8,128)(2,1)} %bitcast.56, bf16[4096,4,128,1]{2,1,0,3:T(4,128)(2,1)} %bitcast.50), kind=kOutput, calls=%fused_computation.4 | convolution fusion | flops 8690589696 | bytes 141590528 | tf_op jit(solution)/shard_map/cond/branch_0_fun/tkgd,rkd->kgtr/dot_general | solution.py:56
  264.5 6.9 %reshape.127 = bf16[4096,4,128]{2,1,0:T(4,128)(2,1)} reshape(bf16[4096,512]{1,0:T(8,128)(2,1)} %get-tuple-element.15) | data formatting | bytes 8388608 | tf_op jit(solution)/shard_map/cond/branch_0_fun/reshape | solution.py:54
  271.4 54.4 %fusion.3 = f32[4,8,256,128]{3,2,1,0:T(8,128)} fusion(f32[4,4096,256,8]{2,1,3,0:T(8,128)} %get-tuple-element.25, f32[4,8,256]{2,1,0:T(8,128)S(1)} %broadcast_maximum_fusion, pred[256,4096]{0,1:T(8,128)(4,1)S(1)} %broadcast_compare_fusion, bf16[4096,4,128,1]{2,1,0,3:T(4,128)(2,1)} %bitcast.51), kind=kOutput, calls=%fused_computation.7 | convolution fusion | flops 8757706752 | bytes 143687680 | tf_op jit(solution)/shard_map/cond/branch_0_fun/kgtr,rkd->kgtd/dot_general | solution.py:64
  325.8 41.3 %fusion.2 = f32[4,8,256]{2,1,0:T(8,128)S(1)} fusion(f32[4,4096,256,8]{2,1,3,0:T(8,128)} %get-tuple-element.25, f32[4,8,256]{2,1,0:T(8,128)S(1)} %broadcast_maximum_fusion, pred[256,4096]{0,1:T(8,128)(4,1)S(1)} %broadcast_compare_fusion), kind=kLoop, calls=%fused_computation.6 | loop fusion | flops 167763968 | bytes 135331840 | tf_op jit(solution)/shard_map/cond/branch_0_fun/reduce_sum | solution.py:63
  367.3 2.9 fusion.21
  370.2 1.4 copy.25
  371.5 2.3 copy.63
  (25 shorter events, 0.1 us)
Async XLA Ops:
  7.2 21.9 %copy-start.5 = (f32[8192]{0:T(1024)S(1)}, f32[8192]{0:T(1024)}, u32[]{:S(2)}) copy-start(f32[8192]{0:T(1024)} %param.14) | copy-start | bytes 98308
  7.2 18.8 %all-gather.4.cloned.1.call-start = ((), (), s32[]{:S(2)}) async-start(), calls=%async_computation.1 | async-start | bytes 6291456 | tf_op jit(solution)/shard_map/all_gather | solution.py:110
  7.9 184.8 %all-gather.6.cloned.1.call-start = ((), (), s32[]{:S(2)}) async-start(), calls=%async_computation.2 | async-start | bytes 4456448 | tf_op jit(solution)/shard_map/all_gather | solution.py:128
  37.9 7.9 %copy-start.6 = (s32[16]{0:T(128)S(1)}, s32[16]{0:T(128)}, u32[]{:S(2)}) copy-start(s32[16]{0:T(128)} %param.21) | copy-start | bytes 196
  37.9 8.1 %copy-start = (bf16[32,8,4,128]{3,1,2,0:T(8,128)(2,1)S(1)}, bf16[32,8,4,128]{3,1,2,0:T(8,128)(2,1)}, u32[]{:S(2)}) copy-start(bf16[32,8,4,128]{3,1,2,0:T(8,128)(2,1)} %copy.64) | copy-start | bytes 786436
  38.0 167.8 %all-gather.8.cloned.1.call-start = ((), (), s32[]{:S(2)}) async-start(), calls=%async_computation.3 | async-start | bytes 4456448 | tf_op jit(solution)/shard_map/all_gather | solution.py:129
  45.8 10.2 %copy-start.3 = (s32[16,62]{1,0:T(8,128)S(1)}, s32[16,62]{1,0:T(8,128)}, u32[]{:S(2)}) copy-start(s32[16,62]{1,0:T(8,128)} %param.22) | copy-start | bytes 11908
  45.8 10.3 %copy-start.2 = (bf16[16,4096]{1,0:T(8,128)(2,1)S(1)}, bf16[16,4096]{1,0:T(8,128)(2,1)}, u32[]{:S(2)}) copy-start(bf16[16,4096]{1,0:T(8,128)(2,1)} %param.20) | copy-start | bytes 393220
  45.8 11.0 %copy-start.4 = (s32[16]{0:T(128)S(1)}, s32[16]{0:T(128)}, u32[]{:S(2)}) copy-start(s32[16]{0:T(128)} %param.23) | copy-start | bytes 196
  49.2 38.6 %all-to-all-start = ((bf16[16,2,16384]{2,1,0:T(2,128)(2,1)}), bf16[16,2,16384]{2,1,0:T(2,128)(2,1)S(1)}, u32[]{:S(2)}, u32[]{:S(2)}) async-start(bf16[16,2,16384]{2,1,0:T(2,128)(2,1)} %reshape.137), calls=%async_computation | async-start | bytes 2097152 | tf_op jit(solution)/shard_map/all_to_all | solution.py:159
  183.6 22.2 %copy-start.1 = (bf16[256,4096]{1,0:T(8,128)(2,1)S(1)}, bf16[256,4096]{1,0:T(8,128)(2,1)}, u32[]{:S(2)}) copy-start(bf16[256,4096]{1,0:T(8,128)(2,1)} %param.17) | copy-start | bytes 6291460
Sparse Core Ops, SparseCore 0:
  9.6 16.3 all-gather.3
  38.1 90.1 all-gather.5
  131.0 74.6 all-gather.7
where the time goes:
time: 383 us; the launch traced here: 380 us
  matrix products  135 us (35%)
  local copies, waits for them, and re-layouts  99.3 us (26%)
  other arithmetic  62.6 us (16%)
  waiting for transfers between devices  61.5 us (16%)
  between operations  14.6 us (4%)
  starting transfers between devices  6.9 us (2%)
    dot_general x1, matrix products, compute(): jnp.einsum('kgtr,rkd->kgtd', weights.astype(jnp.bfloat16), value_block, p...  54.4 us
    dot_general x1, matrix products, compute(): jnp.einsum('tkgd,rkd->kgtr', queries, key_block, preferred_element_type=j...  48.2 us
    reduce_sum x1, other arithmetic, compute(): new_sum = jnp.sum(weights, axis=-1)  41.3 us
    all_to_all x1, waiting for transfers between devices, per_device(): lax.all_to_all(outgoing, 'section', split_axis=0, concat_axis=0, tiled=True)  30.9 us
    reshape x1, local copies, waits for them, and re-layouts, per_device(): cache_keys[block_table].reshape(decode_rows, key_span, kv_heads, head_width)  23.1 us
    reshape x1, local copies, waits for them, and re-layouts, per_device(): cache_values[block_table]  23 us
    all_gather x1, waiting for transfers between devices, per_device(): features = lax.all_gather(prefill_hidden, 'tp', axis=1, tiled=True)  16.8 us
    gather x1, local copies, waits for them, and re-layouts, per_device(): cache_values[block_table]  14.8 us
  transfers between devices with their start and end apart: 4, of which 3 were waited for; matrix products, arithmetic and copies ran while one was open for 31% of the time, Pallas kernels for 0%

commit v1 on v0

v1 whole, which is shorter than its diff:
```python
import functools
import math

import jax
import jax.numpy as jnp
from jax import lax
from jax.experimental import pallas as pl
from jax.experimental.pallas import tpu as pltpu
from jax.sharding import PartitionSpec as P

HD = 128
PAGE = 16
CAP = 2
NORM_EPSILON = 1e-05
ROPE_THETA = 500000.0
LOW = -1e30
EXP2_SCALE = math.log2(math.e) / math.sqrt(HD)
VMEM_BYTES = 56 * 1024 * 1024
NT = (((1,), (1,)), ((), ()))


def params(**kwargs):
    return pltpu.CompilerParams(vmem_limit_bytes=VMEM_BYTES, **kwargs)


def project_kernel(n_parts, chunk, order_ref, *refs):
    parts = refs[:n_parts]
    gain_ref, key_ref, value_ref, cos_ref, sin_ref, out_ref, inv_ref, total_ref = refs[n_parts:]
    step = pl.program_id(0)
    part_width = parts[0].shape[1]
    per_part = part_width // chunk
    width = part_width * n_parts
    key_width = key_ref.shape[1]

    @pl.when(step == 0)
    def _():
        squares = jnp.zeros((parts[0].shape[0], 1), jnp.float32)
        for part in parts:
            for first in range(0, part_width, chunk):
                piece = part[:, first : first + chunk].astype(jnp.float32)
                squares += jnp.sum(piece * piece, axis=1, keepdims=True)
        inverse = lax.rsqrt(squares * (1.0 / width) + NORM_EPSILON)
        inv_ref[...] = jnp.broadcast_to(inverse, inv_ref.shape)
        total_ref[...] = jnp.zeros_like(total_ref)

    for index, part in enumerate(parts):

        @pl.when(step // per_part == index)
        def _(part=part):
            first = pl.multiple_of((step % per_part) * chunk, chunk)
            piece = part[:, pl.ds(first, chunk)].astype(jnp.float32)
            normed = (piece * inv_ref[:, :1] * gain_ref[...]).astype(jnp.bfloat16)
            total_ref[:, :key_width] += jnp.dot(
                normed, key_ref[...], preferred_element_type=jnp.float32
            )
            total_ref[:, key_width:] += jnp.dot(
                normed, value_ref[...], preferred_element_type=jnp.float32
            )

    @pl.when(step == n_parts * per_part - 1)
    def _():
        for head in range(key_width // HD):
            cut = slice(head * HD, (head + 1) * HD)
            raw = total_ref[:, cut]
            turned = raw * cos_ref[...] + pltpu.roll(raw, HD // 2, 1) * sin_ref[...]
            out_ref[:, cut] = turned.astype(jnp.bfloat16)
        out_ref[:, key_width:] = total_ref[:, key_width:].astype(jnp.bfloat16)


def project(parts, order, norm_gain, key_weight, value_weight, cosine, sine):
    rows, part_width = parts[0].shape
    n_parts = len(parts)
    key_width = key_weight.shape[1]
    chunk = math.gcd(part_width, 1024)
    per_part = part_width // chunk

    def weight_index(step, order_ref):
        return (order_ref[step // per_part] * per_part + step % per_part, 0)

    def gain_index(step, order_ref):
        return (0, order_ref[step // per_part] * per_part + step % per_part)

    def whole(step, order_ref):
        return (0, 0)

    return pl.pallas_call(
        functools.partial(project_kernel, n_parts, chunk),
        out_shape=jax.ShapeDtypeStruct((rows, 2 * key_width), jnp.bfloat16),
        grid_spec=pltpu.PrefetchScalarGridSpec(
            num_scalar_prefetch=1,
            grid=(n_parts * per_part,),
            in_specs=[pl.BlockSpec((rows, part_width), whole)] * n_parts
            + [
                pl.BlockSpec((1, chunk), gain_index),
                pl.BlockSpec((chunk, key_width), weight_index),
                pl.BlockSpec((chunk, key_width), weight_index),
                pl.BlockSpec((rows, HD), whole),
                pl.BlockSpec((rows, HD), whole),
            ],
            out_specs=pl.BlockSpec((rows, 2 * key_width), whole),
            scratch_shapes=[
                pltpu.VMEM((rows, HD), jnp.float32),
                pltpu.VMEM((rows, 2 * key_width), jnp.float32),
            ],
        ),
        compiler_params=params(),
        cost_estimate=pl.CostEstimate(
            flops=4 * rows * key_width * part_width * n_parts,
            bytes_accessed=4 * key_width * part_width * n_parts,
            transcendentals=0,
        ),
        name="project",
    )(order, *parts, norm_gain.reshape(1, -1), key_weight, value_weight, cosine, sine)


def stack_heads(ref, group):
    return jnp.concatenate([ref[:, h * HD : (h + 1) * HD] for h in range(group)], axis=0)


def with_ones(values):
    return jnp.concatenate([values, jnp.ones_like(values)], axis=1)


def join_stats(row_max, row_sum):
    lanes = lax.broadcasted_iota(jnp.int32, (row_max.shape[0], HD), 1)
    return jnp.where(lanes < HD // 2, row_max, row_sum)


def counted_piece(queries, keys, values_ones, counts, old_max):
    scores = lax.dot_general(queries, keys, NT, preferred_element_type=jnp.float32)
    counts = jnp.concatenate([counts] * (queries.shape[0] // counts.shape[0]), axis=0)
    scores = jnp.where(counts > 0, scores * EXP2_SCALE, LOW)
    new_max = jnp.maximum(old_max, jnp.max(scores, axis=1, keepdims=True))
    weights = jnp.where(counts > 0, jnp.exp2(scores - new_max) * counts, 0.0)
    product = jnp.dot(
        weights.astype(jnp.bfloat16), values_ones, preferred_element_type=jnp.float32
    )
    return new_max, product


def resident_kernel(group, query_ref, key_ref, value_ref, count_ref, acc_ref, stat_ref):
    queries = stack_heads(query_ref, group)
    rows = queries.shape[0]
    new_max, product = counted_piece(
        queries,
        key_ref[...],
        with_ones(value_ref[...]),
        count_ref[...],
        jnp.full((rows, 1), LOW, jnp.float32),
    )
    acc_ref[0] = product[:, :HD]
    stat_ref[0] = join_stats(new_max, product[:, HD:])


def resident_attention(decode_query, keys, values, counts):
    rows, query_width = decode_query.shape
    pool_rows, key_width = keys.shape
    kv_heads = key_width // HD
    group = query_width // key_width
    state = jax.ShapeDtypeStruct((kv_heads, group * rows, HD), jnp.float32)
    return pl.pallas_call(
        functools.partial(resident_kernel, group),
        out_shape=(state, state),
        grid=(kv_heads,),
        in_specs=[
            pl.BlockSpec((rows, group * HD), lambda g: (0, g)),
            pl.BlockSpec((pool_rows, HD), lambda g: (0, g)),
            pl.BlockSpec((pool_rows, HD), lambda g: (0, g)),
            pl.BlockSpec((rows, pool_rows), lambda g: (0, 0)),
        ],
        out_specs=[pl.BlockSpec((1, group * rows, HD), lambda g: (g, 0, 0))] * 2,
        compiler_params=params(),
        cost_estimate=pl.CostEstimate(
            flops=6 * kv_heads * group * rows * pool_rows * HD,
            bytes_accessed=4 * key_width * pool_rows,
            transcendentals=kv_heads * group * rows * pool_rows,
        ),
        name="resident",
    )(decode_query, keys, values, counts)


def attend_kernel(n_blocks, group, tile_heads, first, final, place_ref, *refs):
    refs = list(refs)

    def take(count):
        taken, refs[:count] = refs[:count], []
        return taken

    query_ref, decode_ref = take(2)
    keys = take(n_blocks)
    values = take(n_blocks)
    counts = take(n_blocks)
    if not first:
        acc_in, stat_in = take(2)
    if final:
        side_acc, side_stat = take(2)
        out_ref, decode_out = take(2)
    else:
        acc_out, stat_out = take(2)
    rows = query_ref.shape[0]
    decode_rows = decode_ref.shape[0]
    own = place_ref[0]
    all_keys = jnp.concatenate([ref[...] for ref in keys], axis=0)
    all_values = jnp.concatenate([with_ones(ref[...]) for ref in values], axis=0)
    seen = [place_ref[1 + b] < own for b in range(n_blocks)]
    tile = tile_heads * rows
    for top in range(0, group * rows, tile):
        heads = range(top // rows, top // rows + tile_heads)
        queries = jnp.concatenate([query_ref[:, h * HD : (h + 1) * HD] for h in heads], axis=0)
        scores = lax.dot_general(queries, all_keys, NT, preferred_element_type=jnp.float32)
        span = scores.shape[1] // n_blocks
        pieces = [scores[:, b * span : (b + 1) * span] for b in range(n_blocks)]
        if first:
            row_of = lax.broadcasted_iota(jnp.int32, (rows, span), 0)
            row_of = jnp.concatenate([row_of] * tile_heads, axis=0)
            column_of = lax.broadcasted_iota(jnp.int32, (tile, span), 1)
            pieces[0] = jnp.where(column_of <= row_of, pieces[0], LOW)
            new_max = jnp.max(pieces[0], axis=1, keepdims=True) * EXP2_SCALE
        else:
            old_max = stat_in[0, top : top + tile, :1]
            new_max = old_max
        for b in range(1 if first else 0, n_blocks):
            highest = jnp.max(pieces[b], axis=1, keepdims=True) * EXP2_SCALE
            new_max = jnp.maximum(new_max, jnp.where(seen[b], highest, LOW))
        weights = []
        for b in range(n_blocks):
            shift = new_max
            if not (first and b == 0):
                shift = new_max + jnp.where(seen[b], 0.0, -LOW)
            weights.append(jnp.exp2(pieces[b] * EXP2_SCALE - shift).astype(jnp.bfloat16))
        product = jnp.dot(
            jnp.concatenate(weights, axis=1), all_values, preferred_element_type=jnp.float32
        )
        acc, total = product[:, :HD], product[:, HD:]
        if not first:
            fade = jnp.exp2(old_max - new_max)
            acc += acc_in[0, top : top + tile, :] * fade
            total += stat_in[0, top : top + tile, HD // 2 : HD // 2 + 1] * fade
        if final:
            result = (acc / total).astype(jnp.bfloat16)
            for place, h in enumerate(heads):
                out_ref[:, h * HD : (h + 1) * HD] = result[place * rows : (place + 1) * rows]
        else:
            acc_out[0, top : top + tile, :] = acc
            stat_out[0, top : top + tile, :] = join_stats(new_max, total)

    queries = stack_heads(decode_ref, group)
    base = group * rows
    small = group * decode_rows
    if first:
        old_max = jnp.full((small, 1), LOW, jnp.float32)
    else:
        old_max = stat_in[0, base : base + small, :1]
    new_max, product = counted_piece(
        queries,
        all_keys,
        all_values,
        jnp.concatenate([ref[...] for ref in counts], axis=1),
        old_max,
    )
    acc, total = product[:, :HD], product[:, HD:]
    if not first:
        fade = jnp.exp2(old_max - new_max)
        acc += acc_in[0, base : base + small, :] * fade
        total += stat_in[0, base : base + small, HD // 2 : HD // 2 + 1] * fade
    if final:
        side_max = side_stat[0, :, :1]
        side_sum = side_stat[0, :, HD // 2 : HD // 2 + 1]
        top_max = jnp.maximum(new_max, side_max)
        fade, side_fade = jnp.exp2(new_max - top_max), jnp.exp2(side_max - top_max)
        acc = acc * fade + side_acc[0] * side_fade
        total = total * fade + side_sum * side_fade
        result = (acc / total).astype(jnp.bfloat16)
        for h in range(group):
            decode_out[:, h * HD : (h + 1) * HD] = result[h * decode_rows : (h + 1) * decode_rows]
    else:
        acc_out[0, base : base + small, :] = acc
        stat_out[0, base : base + small, :] = join_stats(new_max, total)


def attend(place, query, decode_query, blocks, counts, state, side, kv_heads):
    n_blocks = len(blocks)
    rows, query_width = query.shape
    decode_rows = decode_query.shape[0]
    block_rows = blocks[0].shape[0]
    group = query_width // (kv_heads * HD)
    first, final = state is None, side is not None
    total_rows = group * (rows + decode_rows)
    state_spec = pl.BlockSpec((1, total_rows, HD), lambda g, place_ref: (g, 0, 0))
    side_spec = pl.BlockSpec((1, group * decode_rows, HD), lambda g, place_ref: (g, 0, 0))
    query_spec = pl.BlockSpec((rows, group * HD), lambda g, place_ref: (0, g))
    decode_spec = pl.BlockSpec((decode_rows, group * HD), lambda g, place_ref: (0, g))
    key_spec = pl.BlockSpec((block_rows, HD), lambda g, place_ref: (0, g))
    value_spec = pl.BlockSpec((block_rows, HD), lambda g, place_ref: (0, kv_heads + g))
    count_specs = [
        pl.BlockSpec((decode_rows, block_rows), lambda g, place_ref, b=b: (0, place_ref[1 + b]))
        for b in range(n_blocks)
    ]
    operands = [query, decode_query, *blocks, *blocks, *([counts] * n_blocks)]
    in_specs = [query_spec, decode_spec] + [key_spec] * n_blocks + [value_spec] * n_blocks
    in_specs += count_specs
    if not first:
        operands += list(state)
        in_specs += [state_spec] * 2
    if final:
        operands += list(side)
        in_specs += [side_spec] * 2
        out_shape = (
            jax.ShapeDtypeStruct(query.shape, jnp.bfloat16),
            jax.ShapeDtypeStruct(decode_query.shape, jnp.bfloat16),
        )
        out_specs = [query_spec, decode_spec]
    else:
        out_shape = (jax.ShapeDtypeStruct((kv_heads, total_rows, HD), jnp.float32),) * 2
        out_specs = [state_spec] * 2
    tile_heads = math.gcd(group, 2)
    pairs = kv_heads * total_rows * n_blocks * block_rows
    return pl.pallas_call(
        functools.partial(attend_kernel, n_blocks, group, tile_heads, first, final),
        out_shape=out_shape,
        grid_spec=pltpu.PrefetchScalarGridSpec(
            num_scalar_prefetch=1, grid=(kv_heads,), in_specs=in_specs, out_specs=out_specs
        ),
        compiler_params=params(),
        cost_estimate=pl.CostEstimate(
            flops=6 * pairs * HD,
            bytes_accessed=12 * kv_heads * total_rows * HD,
            transcendentals=pairs,
        ),
        name="attend",
    )(place, *operands)


def table_counts(block_table, context_len, cache_pages):
    entries = jnp.arange(block_table.shape[1], dtype=jnp.int32)[None, :]
    length = context_len[:, None]
    whole = (entries + 1) * PAGE <= length
    cut = (entries * PAGE < length) & jnp.logical_not(whole)
    same = block_table[:, :, None] == cache_pages[None, None, :]
    whole_count = jnp.sum((same & whole[:, :, None]).astype(jnp.float32), axis=1)
    cut_count = jnp.sum((same & cut[:, :, None]).astype(jnp.float32), axis=1)
    return whole_count, cut_count


def token_counts(whole_count, cut_count, context_len):
    rows, pages = whole_count.shape
    page_of = jnp.arange(pages * PAGE, dtype=jnp.int32) // PAGE
    spread = (jnp.arange(pages, dtype=jnp.int32)[:, None] == page_of[None, :]).astype(jnp.bfloat16)
    stacked = jnp.concatenate([whole_count, cut_count], axis=0).astype(jnp.bfloat16)
    tokens = jnp.dot(stacked, spread, preferred_element_type=jnp.float32)
    place = jnp.arange(pages * PAGE, dtype=jnp.int32)[None, :] % PAGE
    kept = place < (context_len % PAGE)[:, None]
    return tokens[:rows] + jnp.where(kept, tokens[rows:], 0.0)


def incoming_pages(page_owner, section_count):
    pages = page_owner.shape[0]
    page_index = jnp.arange(pages, dtype=jnp.int32)
    earlier = (page_owner[:, None] == page_owner[None, :]) & (
        page_index[None, :] < page_index[:, None]
    )
    rank = jnp.sum(earlier.astype(jnp.int32), axis=1)
    owners = jnp.arange(section_count, dtype=jnp.int32)
    slots = jnp.arange(CAP, dtype=jnp.int32)
    match = (page_owner[None, None, :] == owners[:, None, None]) & (
        rank[None, None, :] == slots[None, :, None]
    )
    sent = jnp.sum(jnp.where(match, page_index[None, None, :] + 1, 0), axis=2) - 1
    return lax.all_to_all(sent, "section", split_axis=0, concat_axis=0, tiled=True)


def fence(*arrays):
    return lax.optimization_barrier(arrays)


def gather_rounds(own):
    size_z, size_y, size_x = 4, 2, 2
    here = lax.axis_index("section")
    z, column = here // 4, here % 4

    def index(zz, yy, xx):
        return (zz * size_y + yy) * size_x + xx

    def along_z(pairs):
        return [
            (index(a, yy, xx), index(b, yy, xx))
            for a, b in pairs
            for yy in range(size_y)
            for xx in range(size_x)
        ]

    every = [(zz, yy, xx) for zz in range(size_z) for yy in range(size_y) for xx in range(size_x)]
    swap_x = [(index(zz, yy, xx), index(zz, yy, 1 - xx)) for zz, yy, xx in every]
    swap_y = [(index(zz, yy, xx), index(zz, 1 - yy, xx)) for zz, yy, xx in every]
    ends = along_z([(0, 1), (1, 0), (2, 3), (3, 2)])
    middle = along_z([(1, 2), (2, 1)])
    outward = along_z([(1, 0), (2, 3)])
    inward = along_z([(0, 1), (3, 2)])
    inner = (z == 1) | (z == 2)

    def move(block, pairs):
        return lax.ppermute(block, "section", pairs)

    plane_a = jnp.bitwise_xor(z, 1)
    plane_f = jnp.where(inner, 3 - z, jnp.where(z == 0, 2, 1))
    plane_g = jnp.where(inner, jnp.bitwise_xor(3 - z, 1), 3 - z)

    def at(plane, turn):
        return plane * 4 + jnp.bitwise_xor(column, turn)

    own_x, own_y, a, b = fence(
        move(own, swap_x), move(own, swap_y), move(own, ends), move(own, middle)
    )
    rounds = [[(own, here), (own_x, at(z, 1)), (own_y, at(z, 2)), (a, at(plane_a, 0))]]
    yield rounds[-1]
    own_d, a_y, c, d = fence(
        move(own_y, swap_x), move(a, swap_y), move(b, outward), move(a, middle)
    )
    f = jnp.where(inner, b, c)
    yield [(own_d, at(z, 3)), (a_y, at(plane_a, 2)), (f, at(plane_f, 0))]
    a_x, f_y, e, a_in, b_in = fence(
        move(a, swap_x),
        move(f, swap_y),
        move(d, outward),
        move(own_d, inward),
        move(own_d, middle),
    )
    g = jnp.where(inner, d, e)
    yield [(a_x, at(plane_a, 1)), (f_y, at(plane_f, 2)), (g, at(plane_g, 0))]
    f_x, g_y, c_in, d_in = fence(
        move(f, swap_x), move(g, swap_y), move(b_in, outward), move(a_in, middle)
    )
    f_d = jnp.where(inner, b_in, c_in)
    yield [(f_x, at(plane_f, 1)), (g_y, at(plane_g, 2)), (f_d, at(plane_f, 3))]
    g_x, a_turn, e_in = fence(move(g, swap_x), move(a_x, swap_y), move(d_in, outward))
    a_d = jnp.where(inner, a_in, a_turn)
    g_d = jnp.where(inner, d_in, e_in)
    yield [(g_x, at(plane_g, 1)), (a_d, at(plane_a, 3)), (g_d, at(plane_g, 3))]


def gather_plain(own, section_count):
    rows = own.shape[0]
    gathered = lax.all_gather(own, "section", axis=0, tiled=True)
    step = math.gcd(section_count, 4)
    for top in range(0, section_count, step):
        yield [
            (gathered[s * rows : (s + 1) * rows], jnp.int32(s)) for s in range(top, top + step)
        ]


def per_device(
    prefill_hidden,
    norm_gain,
    key_weight,
    value_weight,
    prefill_query,
    resident_keys,
    resident_values,
    decode_query,
    page_owner,
    block_table,
    context_len,
):
    section_count = lax.axis_size("section")
    tp_count = lax.axis_size("tp")
    section = lax.axis_index("section").astype(jnp.int32)
    tp = lax.axis_index("tp").astype(jnp.int32)
    rows = prefill_hidden.shape[0]
    key_width = key_weight.shape[1]
    kv_heads = key_width // HD
    pool = resident_keys.shape[0]

    if tp_count == 2:
        other = lax.ppermute(prefill_hidden, "tp", [(0, 1), (1, 0)])
        parts, order = [prefill_hidden, other], jnp.stack([tp, 1 - tp])
    else:
        parts = [lax.all_gather(prefill_hidden, "tp", axis=1, tiled=True)]
        order = jnp.zeros((1,), jnp.int32)

    half = HD // 2
    frequency = jnp.exp(jnp.arange(half, dtype=jnp.float32) * (-2.0 * math.log(ROPE_THETA) / HD))
    positions = section * rows + jnp.arange(rows, dtype=jnp.int32)
    angles = positions.astype(jnp.float32)[:, None] * frequency[None, :]
    cosine, sine = jnp.cos(angles), jnp.sin(angles)
    cosine = jnp.concatenate([cosine, cosine], axis=1)
    sine = jnp.concatenate([-sine, sine], axis=1)

    own = project(parts, order, norm_gain, key_weight, value_weight, cosine, sine)

    slot_pages = incoming_pages(page_owner, section_count).reshape(-1)
    resident_ids = jnp.arange(pool, dtype=jnp.int32)
    resident_count = token_counts(
        *table_counts(block_table, context_len, resident_ids), context_len
    )
    side = resident_attention(
        decode_query,
        resident_keys.reshape(pool * PAGE, key_width),
        resident_values.reshape(pool * PAGE, key_width),
        resident_count,
    )
    slot_ids = pool + jnp.arange(section_count * CAP, dtype=jnp.int32)
    slot_whole, slot_cut = table_counts(block_table, context_len, slot_ids)
    pages_here = rows // PAGE
    slot_page = jnp.where(
        slot_pages >= 0,
        jnp.arange(section_count * CAP, dtype=jnp.int32) // CAP * pages_here + slot_pages,
        -1,
    )
    pages_all = jnp.arange(section_count * pages_here, dtype=jnp.int32)
    fills = (slot_page[:, None] == pages_all[None, :]).astype(jnp.float32)
    prompt_count = token_counts(
        jnp.dot(slot_whole, fills, precision=lax.Precision.HIGHEST),
        jnp.dot(slot_cut, fills, precision=lax.Precision.HIGHEST),
        context_len,
    )

    if section_count == 16:
        rounds = gather_rounds(own)
        n_rounds, state = 5, None
        later_count = prompt_count
    else:
        first_place = jnp.stack([section, section])
        state = attend(
            first_place, prefill_query, decode_query, [own], prompt_count, None, None, kv_heads
        )
        rounds = gather_plain(own, section_count)
        n_rounds = section_count // math.gcd(section_count, 4)
        mine = jnp.arange(section_count * rows, dtype=jnp.int32) // rows == section
        later_count = jnp.where(mine[None, :], 0.0, prompt_count)
    for number, arrived in enumerate(rounds):
        place = jnp.stack([section] + [s.astype(jnp.int32) for _, s in arrived])
        state = attend(
            place,
            prefill_query,
            decode_query,
            [block for block, _ in arrived],
            later_count,
            state,
            side if number == n_rounds - 1 else None,
            kv_heads,
        )
    return state


def solution(mesh):
    return jax.shard_map(
        per_device,
        mesh=mesh,
        in_specs=(
            P("section", "tp"),
            P(),
            P(None, "tp"),
            P(None, "tp"),
            P("section", "tp"),
            P("section", None, "tp"),
            P("section", None, "tp"),
            P("section", "tp"),
            P("section"),
            P("section", None),
            P("section"),
        ),
        out_specs=(P("section", "tp"), P("section", "tp")),
        check_vma=False,
    )
```

time: 383 us -> 198 us (0.52)
  matrix products: 135 us -> 2.02 us
  Pallas kernels: 0 us -> 126 us
  local copies, waits for them, and re-layouts: 99.3 us -> 4.3 us
  other arithmetic: 62.6 us -> 13.1 us
  waiting for transfers between devices: 61.5 us -> 15.1 us
  starting transfers between devices: 6.9 us -> 34.2 us
  between operations: 14.6 us -> 1.27 us
    dot_general x7 -> x4, matrix products: 135 us -> 2.02 us  [the longest x2 1.62 us: token_counts(): tokens = jnp.dot(stacked, spread, preferred_element_type=jnp.float32)]
    pallas_call x0 -> x7, Pallas kernels: none -> 126 us  [the longest x5 102 us: attend(): pl.pallas_call(functools.partial(attend_kernel, n_blocks, group, tile_hea...]
    reshape x8 -> x1, local copies, waits for them, and re-layouts: 62.7 us -> 0.08 us  [per_device(): slot_pages = incoming_pages(page_owner, section_count).reshape(-1)]
    reduce_sum x4, other arithmetic: 45.2 us -> 2.68 us  [the longest x2 1.65 us: table_counts(): jnp.sum((same & whole[:, :, None]).astype(jnp.float32), axis=1)]
    all_to_all x1, waiting for transfers between devices: 30.9 us -> 0.01 us  [incoming_pages(): lax.all_to_all(sent, 'section', split_axis=0, concat_axis=0, tiled=True)]
    all_gather x3 -> x0, waiting for transfers between devices: 29.9 us -> none  [the longest x1 16.8 us: per_device(): features = lax.all_gather(prefill_hidden, 'tp', axis=1, tiled=True)]
    gather x2 -> x0, local copies, waits for them, and re-layouts: 29.4 us -> none  [the longest x1 14.8 us: per_device(): cache_values[block_table]]
    ppermute x0 -> x21, starting transfers between devices: none -> 26.3 us  [the longest x20 25.8 us: move(): return lax.ppermute(block, 'section', pairs)]
  transfers between devices with their start and end apart: 4 -> 22, of which waited for: 3 -> 4; matrix products, arithmetic and copies ran while one was open for 31% -> 9% of each run, Pallas kernels for 0% -> 47%
where the time goes in v1:
time: 198 us; the launch traced here: 196 us
  Pallas kernels  126 us (64%)
  starting transfers between devices  34.2 us (17%)
  waiting for transfers between devices  15.1 us (8%)
  other arithmetic  13.1 us (7%)
  local copies, waits for them, and re-layouts  4.3 us (2%)
  matrix products  2.02 us (1%)
    pallas_call x5, Pallas kernels, attend(): pl.pallas_call(functools.partial(attend_kernel, n_blocks, group, tile_hea...  102 us
    ppermute x20, starting transfers between devices, move(): return lax.ppermute(block, 'section', pairs)  25.8 us
    ppermute x20, waiting for transfers between devices, move(): return lax.ppermute(block, 'section', pairs)  15.1 us
    pallas_call x1, Pallas kernels, project(): pl.pallas_call(functools.partial(project_kernel, n_parts, chunk), out_sha...  14.6 us
    pallas_call x1, Pallas kernels, resident_attention(): pl.pallas_call(functools.partial(resident_kernel, group), out_shape=(stat...  8.99 us
    all_to_all x1, starting transfers between devices, incoming_pages(): lax.all_to_all(sent, 'section', split_axis=0, concat_axis=0, tiled=True)  7.88 us
  transfers between devices with their start and end apart: 22, of which 4 were waited for; matrix products, arithmetic and copies ran while one was open for 9% of the time, Pallas kernels for 47%

profile of v1, /device:TPU:0, one launch (start us, length us, event | category | flops | bytes accessed | tf_op | source)
XLA Modules:
  0.0 195.6 jit_solution(1472631357312431203)
XLA Ops:
  1.1 0.7 iota_compare_fusion.8
  1.8 0.9 convert_reduce_fusion.4
  2.9 0.7 copy.20
  3.5 7.9 %all-to-all-start = ((s32[16,1,2]{2,1,0:T(1,128)}), s32[16,1,2]{2,1,0:T(1,128)S(1)}, u32[]{:S(2)}, u32[]{:S(2)}) async-start(s32[16,1,2]{2,1,0:T(1,128)} %copy.20), calls=%async_computation | async-start | bytes 16384 | tf_op jit(solution)/shard_map/all_to_all | solution.py:369
  11.5 0.7 not_and_fusion
  12.5 0.8 copy.21
  13.3 0.7 pad_add_fusion.1.order_ref
  15.2 0.7 pad_add_fusion.2
  16.4 0.8 pad_maximum_fusion.refs_5_
  17.2 0.8 pad_maximum_fusion.1.refs_6_
  17.9 1.0 convert_reduce_fusion.3
  18.9 0.7 convert_reduce_fusion.1
  19.6 0.7 and_select_fusion
  20.2 0.8 fusion
  22.2 0.7 reduce.3
  23.0 1.3 copy-done
  24.3 14.6 %project.1.refs_2_.refs_6_ = bf16[256,1024]{1,0:T(8,128)(2,1)} custom-call(s32[2]{0:T(128)} %pad_add_fusion.1.order_ref, bf16[256,4096]{1,0:T(8,128)(2,1)} %refs_0_.6, bf16[256,4096]{1,0:T(8,128)(2,1)} %copy-done, f32[1,8192]{1,0:T(1,128)} %bitcast.27, bf16[8192,512]{1,0:T(8,128)(2,1)} %refs_3_.1, bf16[8192,512]{1,0:T(8,128)(2,1)} %refs_4_.1, ...), custom_call_target="tpu_custom_call" | custom-call | flops 4294967296 | bytes 16777216 | tf_op jit(solution)/shard_map/project/pallas_call | solution.py:86
  38.9 1.9 collective-permute-start.1
  40.8 1.4 collective-permute-start.2
  42.3 1.5 collective-permute-start.3
  43.8 0.7 collective-permute-start.4
  44.9 0.8 fusion.1
  45.7 7.5 %collective-permute-done.1.refs_3_.refs_7_ = bf16[256,1024]{1,0:T(8,128)(2,1)S(1)} collective-permute-done((bf16[256,1024]{1,0:T(8,128)(2,1)}, bf16[256,1024]{1,0:T(8,128)(2,1)S(1)}, u32[]{:S(2)}, u32[]{:S(2)}) %collective-permute-start.1) | collective-permute-done | bytes 524320 | tf_op jit(solution)/shard_map/ppermute | solution.py:402
  53.2 1.3 collective-permute-done.2.refs_4_.refs_8_
  54.5 1.2 collective-permute-done.3.refs_5_.refs_9_
  56.3 0.7 collective-permute-start.8
  57.4 1.3 collective-permute-start.7
  58.7 0.9 fusion.7
  59.7 9.0 %resident.1 = (f32[4,128,128]{2,1,0:T(8,128)}, f32[4,128,128]{2,1,0:T(8,128)}) custom-call(bf16[16,4096]{1,0:T(8,128)(2,1)} %refs_1_.9, bf16[4096,512]{1,0:T(8,128)(2,1)} %bitcast.25, bf16[4096,512]{1,0:T(8,128)(2,1)} %bitcast.26, f32[16,4096]{1,0:T(8,128)} %get-tuple-element.66.count_ref), custom_call_target="tpu_custom_call" | custom-call | flops 1610612736 | bytes 8388608 | tf_op jit(solution)/shard_map/resident/pallas_call | solution.py:161
  68.7 1.7 collective-permute-start.9
  70.4 5.1 %collective-permute-done.7 = bf16[256,1024]{1,0:T(8,128)(2,1)S(1)} collective-permute-done((bf16[256,1024]{1,0:T(8,128)(2,1)S(1)}, bf16[256,1024]{1,0:T(8,128)(2,1)S(1)}, u32[]{:S(2)}, u32[]{:S(2)}) %collective-permute-start.7) | collective-permute-done | bytes 524320 | tf_op jit(solution)/shard_map/ppermute | solution.py:402
  75.5 4.1 %collective-permute-start.12 = (bf16[256,1024]{1,0:T(8,128)(2,1)S(1)}, bf16[256,1024]{1,0:T(8,128)(2,1)S(1)}, u32[]{:S(2)}, u32[]{:S(2)}) collective-permute-start(bf16[256,1024]{1,0:T(8,128)(2,1)S(1)} %collective-permute-done.5.refs_2_.refs_5_), channel_id=1, source_target_pairs={{0,8},{2,10},{4,12},{6,14},{24,16},{26,18},{28,20},{30,22},{1,9},{... | collective-permute-start | bytes 1572872 | tf_op jit(solution)/shard_map/ppermute | solution.py:402
  79.6 0.7 collective-permute-start.13
  80.4 1.5 collective-permute-start.10
  81.9 1.5 collective-permute-start.11
  83.3 16.3 %attend.5 = (f32[4,2176,128]{2,1,0:T(8,128)}, f32[4,2176,128]{2,1,0:T(8,128)}) custom-call(s32[5]{0:T(128)} %stack.100.place_ref, bf16[256,4096]{1,0:T(8,128)(2,1)} %refs_0_.11, bf16[16,4096]{1,0:T(8,128)(2,1)} %refs_1_.9, bf16[256,1024]{1,0:T(8,128)(2,1)} %project.1.refs_2_.refs_6_, bf16[256,1024]{1,0:T(8,128)(2,1)} %copy-done.6, ...), custom_call_target="tpu_custom_call" | custom-call | flops 6845104128 | bytes 13369344 | tf_op jit(solution)/shard_map/attend/pallas_call | solution.py:318
  100.4 0.7 collective-permute-start.17
  101.1 1.3 collective-permute-start.18
  102.4 0.7 collective-permute-start.19
  103.1 22.1 %attend.6 = (f32[4,2176,128]{2,1,0:T(8,128)}, f32[4,2176,128]{2,1,0:T(8,128)}) custom-call(s32[4]{0:T(128)} %pad_add_fusion.4.place_ref, bf16[256,4096]{1,0:T(8,128)(2,1)} %refs_0_.11, bf16[16,4096]{1,0:T(8,128)(2,1)} %refs_1_.9, bf16[256,1024]{1,0:T(8,128)(2,1)} %copy-done.8, bf16[256,1024]{1,0:T(8,128)(2,1)} %copy-done.5, bf16[256,1024]{1,0:T(8,128)(2,1)} %copy-done.1, ...), custom_call_target="tpu_custom_call" | custom-call | flops 5133828096 | bytes 13369344 | tf_op jit(solution)/shard_map/attend/pallas_call | solution.py:318
  125.2 1.6 collective-permute-start.14
  126.7 22.1 %attend.7 = (f32[4,2176,128]{2,1,0:T(8,128)}, f32[4,2176,128]{2,1,0:T(8,128)}) custom-call(s32[4]{0:T(128)} %get-tuple-element.74.place_ref, bf16[256,4096]{1,0:T(8,128)(2,1)} %refs_0_.11, bf16[16,4096]{1,0:T(8,128)(2,1)} %refs_1_.9, bf16[256,1024]{1,0:T(8,128)(2,1)} %copy-done.3, bf16[256,1024]{1,0:T(8,128)(2,1)} %copy-done.12, ...), custom_call_target="tpu_custom_call" | custom-call | flops 5133828096 | bytes 13369344 | tf_op jit(solution)/shard_map/attend/pallas_call | solution.py:318
  148.9 1.5 collective-permute-start.15
  150.3 1.5 collective-permute-start.20
  151.9 0.8 broadcast_select_fusion.refs_4_.refs_7_
  152.7 22.0 %attend.8 = (f32[4,2176,128]{2,1,0:T(8,128)}, f32[4,2176,128]{2,1,0:T(8,128)}) custom-call(s32[4]{0:T(128)} %get-tuple-element.73.place_ref, bf16[256,4096]{1,0:T(8,128)(2,1)} %refs_0_.11, bf16[16,4096]{1,0:T(8,128)(2,1)} %refs_1_.9, bf16[256,1024]{1,0:T(8,128)(2,1)} %copy-done.10, bf16[256,1024]{1,0:T(8,128)(2,1)} %copy-done.13, ...), custom_call_target="tpu_custom_call" | custom-call | flops 5133828096 | bytes 13369344 | tf_op jit(solution)/shard_map/attend/pallas_call | solution.py:318
  174.8 1.1 broadcast_select_fusion.1
  175.9 19.5 %attend.9 = (bf16[256,4096]{1,0:T(8,128)(2,1)}, bf16[16,4096]{1,0:T(8,128)(2,1)}) custom-call(s32[4]{0:T(128)} %pad_add_fusion.place_ref, bf16[256,4096]{1,0:T(8,128)(2,1)} %refs_0_.11, bf16[16,4096]{1,0:T(8,128)(2,1)} %refs_1_.9, bf16[256,1024]{1,0:T(8,128)(2,1)} %copy-done.11, bf16[256,1024]{1,0:T(8,128)(2,1)} %get-tuple-element.76.refs_3_.refs_6_, ...), custom_call_target="tpu_custom_call" | custom-call | flops 5133828096 | bytes 13369344 | tf_op jit(solution)/shard_map/attend/pallas_call | solution.py:318
  (72 shorter events, 6.2 us)
Async XLA Ops:
  0.6 22.3 %collective-permute-start = (bf16[256,4096]{1,0:T(8,128)(2,1)}, bf16[256,4096]{1,0:T(8,128)(2,1)S(1)}, u32[]{:S(2)}, u32[]{:S(2)}) collective-permute-start(bf16[256,4096]{1,0:T(8,128)(2,1)} %refs_0_.6), channel_id=1, source_target_pairs={{0,1},{1,0},{2,3},{3,2},{4,5},{5,4},{6,7},{7,6},{8,9},{9,8},{10,11... | collective-permute-start | bytes 6291464 | tf_op jit(solution)/shard_map/ppermute | solution.py:474
  3.5 18.1 %all-to-all-start = ((s32[16,1,2]{2,1,0:T(1,128)}), s32[16,1,2]{2,1,0:T(1,128)S(1)}, u32[]{:S(2)}, u32[]{:S(2)}) async-start(s32[16,1,2]{2,1,0:T(1,128)} %copy.20), calls=%async_computation | async-start | bytes 16384 | tf_op jit(solution)/shard_map/all_to_all | solution.py:369
  23.0 1.3 copy-start
  38.9 14.3 %collective-permute-start.1 = (bf16[256,1024]{1,0:T(8,128)(2,1)}, bf16[256,1024]{1,0:T(8,128)(2,1)S(1)}, u32[]{:S(2)}, u32[]{:S(2)}) collective-permute-start(bf16[256,1024]{1,0:T(8,128)(2,1)} %project.1.refs_2_.refs_6_), channel_id=1, source_target_pairs={{0,2},{2,0},{4,6},{6,4},{8,10},{10,8},{12,14},{14,12},{16,18},{18,... | collective-permute-start | bytes 1572872 | tf_op jit(solution)/shard_map/ppermute | solution.py:402
  40.8 13.7 %collective-permute-start.2 = (bf16[256,1024]{1,0:T(8,128)(2,1)}, bf16[256,1024]{1,0:T(8,128)(2,1)S(1)}, u32[]{:S(2)}, u32[]{:S(2)}) collective-permute-start(bf16[256,1024]{1,0:T(8,128)(2,1)} %project.1.refs_2_.refs_6_), channel_id=1, source_target_pairs={{0,4},{2,6},{4,0},{6,2},{8,12},{10,14},{12,8},{14,10},{16,20},{18,... | collective-permute-start | bytes 1572872 | tf_op jit(solution)/shard_map/ppermute | solution.py:402
  42.3 13.4 %collective-permute-start.3 = (bf16[256,1024]{1,0:T(8,128)(2,1)}, bf16[256,1024]{1,0:T(8,128)(2,1)S(1)}, u32[]{:S(2)}, u32[]{:S(2)}) collective-permute-start(bf16[256,1024]{1,0:T(8,128)(2,1)} %project.1.refs_2_.refs_6_), channel_id=1, source_target_pairs={{0,8},{2,10},{4,12},{6,14},{8,0},{10,2},{12,4},{14,6},{16,24},{18,... | collective-permute-start | bytes 1572872 | tf_op jit(solution)/shard_map/ppermute | solution.py:402
  43.8 11.9 %collective-permute-start.4 = (bf16[256,1024]{1,0:T(8,128)(2,1)}, bf16[256,1024]{1,0:T(8,128)(2,1)S(1)}, u32[]{:S(2)}, u32[]{:S(2)}) collective-permute-start(bf16[256,1024]{1,0:T(8,128)(2,1)} %project.1.refs_2_.refs_6_), channel_id=1, source_target_pairs={{8,16},{10,18},{12,20},{14,22},{16,8},{18,10},{20,12},{22,14},{9,1... | collective-permute-start | bytes 1572872 | tf_op jit(solution)/shard_map/ppermute | solution.py:402
  53.2 15.5 %copy-start.6 = (bf16[256,1024]{1,0:T(8,128)(2,1)}, bf16[256,1024]{1,0:T(8,128)(2,1)S(1)}, u32[]{:S(2)}) copy-start(bf16[256,1024]{1,0:T(8,128)(2,1)S(1)} %collective-permute-done.1.refs_3_.refs_7_) | copy-start | bytes 1572868
  54.5 14.1 %copy-start.7 = (bf16[256,1024]{1,0:T(8,128)(2,1)}, bf16[256,1024]{1,0:T(8,128)(2,1)S(1)}, u32[]{:S(2)}) copy-start(bf16[256,1024]{1,0:T(8,128)(2,1)S(1)} %collective-permute-done.2.refs_4_.refs_8_) | copy-start | bytes 1572868
  55.7 13.0 %copy-start.9 = (bf16[256,1024]{1,0:T(8,128)(2,1)}, bf16[256,1024]{1,0:T(8,128)(2,1)S(1)}, u32[]{:S(2)}) copy-start(bf16[256,1024]{1,0:T(8,128)(2,1)S(1)} %collective-permute-done.3.refs_5_.refs_9_) | copy-start | bytes 1572868
  55.7 14.6 %collective-permute-start.6 = (bf16[256,1024]{1,0:T(8,128)(2,1)S(1)}, bf16[256,1024]{1,0:T(8,128)(2,1)S(1)}, u32[]{:S(2)}, u32[]{:S(2)}) collective-permute-start(bf16[256,1024]{1,0:T(8,128)(2,1)S(1)} %collective-permute-done.3.refs_5_.refs_9_), channel_id=1, source_target_pairs={{0,4},{2,6},{4,0},{6,2},{8,12},{10,14},{12,8},{14,10},{16,20},{18,... | collective-permute-start | bytes 1572872 | tf_op jit(solution)/shard_map/ppermute | solution.py:402
  56.3 14.1 %collective-permute-start.8 = (bf16[256,1024]{1,0:T(8,128)(2,1)S(1)}, bf16[256,1024]{1,0:T(8,128)(2,1)S(1)}, u32[]{:S(2)}, u32[]{:S(2)}) collective-permute-start(bf16[256,1024]{1,0:T(8,128)(2,1)S(1)} %collective-permute-done.3.refs_5_.refs_9_), channel_id=1, source_target_pairs={{8,16},{10,18},{12,20},{14,22},{16,8},{18,10},{20,12},{22,14},{9,1... | collective-permute-start | bytes 1572872 | tf_op jit(solution)/shard_map/ppermute | solution.py:402
  57.0 13.4 %collective-permute-start.5 = (bf16[256,1024]{1,0:T(8,128)(2,1)S(1)}, bf16[256,1024]{1,0:T(8,128)(2,1)S(1)}, u32[]{:S(2)}, u32[]{:S(2)}) collective-permute-start(bf16[256,1024]{1,0:T(8,128)(2,1)S(1)} %collective-permute-done.2.refs_4_.refs_8_), channel_id=1, source_target_pairs={{0,2},{2,0},{4,6},{6,4},{8,10},{10,8},{12,14},{14,12},{16,18},{18,... | collective-permute-start | bytes 1572872 | tf_op jit(solution)/shard_map/ppermute | solution.py:402
  57.4 18.0 %collective-permute-start.7 = (bf16[256,1024]{1,0:T(8,128)(2,1)S(1)}, bf16[256,1024]{1,0:T(8,128)(2,1)S(1)}, u32[]{:S(2)}, u32[]{:S(2)}) collective-permute-start(bf16[256,1024]{1,0:T(8,128)(2,1)S(1)} %collective-permute-done.4), channel_id=1, source_target_pairs={{8,0},{10,2},{12,4},{14,6},{16,24},{18,26},{20,28},{22,30},{9,1},{... | collective-permute-start | bytes 1572872 | tf_op jit(solution)/shard_map/ppermute | solution.py:402
  68.7 31.0 %collective-permute-start.9 = (bf16[256,1024]{1,0:T(8,128)(2,1)S(1)}, bf16[256,1024]{1,0:T(8,128)(2,1)S(1)}, u32[]{:S(2)}, u32[]{:S(2)}) collective-permute-start(bf16[256,1024]{1,0:T(8,128)(2,1)S(1)} %collective-permute-done.3.refs_5_.refs_9_), channel_id=1, source_target_pairs={{0,2},{2,0},{4,6},{6,4},{8,10},{10,8},{12,14},{14,12},{16,18},{18,... | collective-permute-start | bytes 1572872 | tf_op jit(solution)/shard_map/ppermute | solution.py:402
  70.3 29.3 %copy-start.5 = (bf16[256,1024]{1,0:T(8,128)(2,1)}, bf16[256,1024]{1,0:T(8,128)(2,1)S(1)}, u32[]{:S(2)}) copy-start(bf16[256,1024]{1,0:T(8,128)(2,1)S(1)} %collective-permute-done.6.refs_3_.refs_6_) | copy-start | bytes 1572868
  70.4 29.3 %copy-start.8 = (bf16[256,1024]{1,0:T(8,128)(2,1)}, bf16[256,1024]{1,0:T(8,128)(2,1)S(1)}, u32[]{:S(2)}) copy-start(bf16[256,1024]{1,0:T(8,128)(2,1)S(1)} %collective-permute-done.5.refs_2_.refs_5_) | copy-start | bytes 1572868
  75.5 24.8 %collective-permute-start.12 = (bf16[256,1024]{1,0:T(8,128)(2,1)S(1)}, bf16[256,1024]{1,0:T(8,128)(2,1)S(1)}, u32[]{:S(2)}, u32[]{:S(2)}) collective-permute-start(bf16[256,1024]{1,0:T(8,128)(2,1)S(1)} %collective-permute-done.5.refs_2_.refs_5_), channel_id=1, source_target_pairs={{0,8},{2,10},{4,12},{6,14},{24,16},{26,18},{28,20},{30,22},{1,9},{... | collective-permute-start | bytes 1572872 | tf_op jit(solution)/shard_map/ppermute | solution.py:402
  79.6 20.7 %collective-permute-start.13 = (bf16[256,1024]{1,0:T(8,128)(2,1)S(1)}, bf16[256,1024]{1,0:T(8,128)(2,1)S(1)}, u32[]{:S(2)}, u32[]{:S(2)}) collective-permute-start(bf16[256,1024]{1,0:T(8,128)(2,1)S(1)} %collective-permute-done.5.refs_2_.refs_5_), channel_id=1, source_target_pairs={{8,16},{10,18},{12,20},{14,22},{16,8},{18,10},{20,12},{22,14},{9,1... | collective-permute-start | bytes 1572872 | tf_op jit(solution)/shard_map/ppermute | solution.py:402
  80.4 19.3 %copy-start.1 = (bf16[256,1024]{1,0:T(8,128)(2,1)}, bf16[256,1024]{1,0:T(8,128)(2,1)S(1)}, u32[]{:S(2)}) copy-start(bf16[256,1024]{1,0:T(8,128)(2,1)S(1)} %broadcast_select_fusion.4.refs_4_.refs_7_) | copy-start | bytes 1572868
  80.4 19.9 %collective-permute-start.10 = (bf16[256,1024]{1,0:T(8,128)(2,1)S(1)}, bf16[256,1024]{1,0:T(8,128)(2,1)S(1)}, u32[]{:S(2)}, u32[]{:S(2)}) collective-permute-start(bf16[256,1024]{1,0:T(8,128)(2,1)S(1)} %broadcast_select_fusion.4.refs_4_.refs_7_), channel_id=1, source_target_pairs={{0,4},{2,6},{4,0},{6,2},{8,12},{10,14},{12,8},{14,10},{16,20},{18,... | collective-permute-start | bytes 1572872 | tf_op jit(solution)/shard_map/ppermute | solution.py:402
  81.9 18.4 %collective-permute-start.11 = (bf16[256,1024]{1,0:T(8,128)(2,1)S(1)}, bf16[256,1024]{1,0:T(8,128)(2,1)S(1)}, u32[]{:S(2)}, u32[]{:S(2)}) collective-permute-start(bf16[256,1024]{1,0:T(8,128)(2,1)S(1)} %collective-permute-done.8), channel_id=1, source_target_pairs={{8,0},{10,2},{12,4},{14,6},{16,24},{18,26},{20,28},{22,30},{9,1},{... | collective-permute-start | bytes 1572872 | tf_op jit(solution)/shard_map/ppermute | solution.py:402
  99.7 25.5 %copy-start.3 = (bf16[256,1024]{1,0:T(8,128)(2,1)}, bf16[256,1024]{1,0:T(8,128)(2,1)S(1)}, u32[]{:S(2)}) copy-start(bf16[256,1024]{1,0:T(8,128)(2,1)S(1)} %collective-permute-done.9.refs_2_.refs_5_) | copy-start | bytes 1572868
  99.7 49.2 %collective-permute-start.16 = (bf16[256,1024]{1,0:T(8,128)(2,1)S(1)}, bf16[256,1024]{1,0:T(8,128)(2,1)S(1)}, u32[]{:S(2)}, u32[]{:S(2)}) collective-permute-start(bf16[256,1024]{1,0:T(8,128)(2,1)S(1)} %broadcast_select_fusion.4.refs_4_.refs_7_), channel_id=1, source_target_pairs={{0,2},{2,0},{4,6},{6,4},{8,10},{10,8},{12,14},{14,12},{16,18},{18,... | collective-permute-start | bytes 1572872 | tf_op jit(solution)/shard_map/ppermute | solution.py:402
  100.3 24.9 %copy-start.12 = (bf16[256,1024]{1,0:T(8,128)(2,1)}, bf16[256,1024]{1,0:T(8,128)(2,1)S(1)}, u32[]{:S(2)}) copy-start(bf16[256,1024]{1,0:T(8,128)(2,1)S(1)} %collective-permute-done.10.refs_3_.refs_6_) | copy-start | bytes 1572868
  100.4 24.8 %copy-start.2 = (bf16[256,1024]{1,0:T(8,128)(2,1)}, bf16[256,1024]{1,0:T(8,128)(2,1)S(1)}, u32[]{:S(2)}) copy-start(bf16[256,1024]{1,0:T(8,128)(2,1)S(1)} %broadcast_select_fusion.3.refs_4_.refs_7_) | copy-start | bytes 1572868
  100.4 49.9 %collective-permute-start.17 = (bf16[256,1024]{1,0:T(8,128)(2,1)S(1)}, bf16[256,1024]{1,0:T(8,128)(2,1)S(1)}, u32[]{:S(2)}, u32[]{:S(2)}) collective-permute-start(bf16[256,1024]{1,0:T(8,128)(2,1)S(1)} %broadcast_select_fusion.3.refs_4_.refs_7_), channel_id=1, source_target_pairs={{0,4},{2,6},{4,0},{6,2},{8,12},{10,14},{12,8},{14,10},{16,20},{18,... | collective-permute-start | bytes 1572872 | tf_op jit(solution)/shard_map/ppermute | solution.py:402
  101.1 49.3 %collective-permute-start.18 = (bf16[256,1024]{1,0:T(8,128)(2,1)S(1)}, bf16[256,1024]{1,0:T(8,128)(2,1)S(1)}, u32[]{:S(2)}, u32[]{:S(2)}) collective-permute-start(bf16[256,1024]{1,0:T(8,128)(2,1)S(1)} %collective-permute-done.13), channel_id=1, source_target_pairs={{8,0},{10,2},{12,4},{14,6},{16,24},{18,26},{20,28},{22,30},{9,1},{... | collective-permute-start | bytes 1572872 | tf_op jit(solution)/shard_map/ppermute | solution.py:402
  102.4 48.0 %collective-permute-start.19 = (bf16[256,1024]{1,0:T(8,128)(2,1)S(1)}, bf16[256,1024]{1,0:T(8,128)(2,1)S(1)}, u32[]{:S(2)}, u32[]{:S(2)}) collective-permute-start(bf16[256,1024]{1,0:T(8,128)(2,1)S(1)} %collective-permute-done.12), channel_id=1, source_target_pairs={{8,16},{10,18},{12,20},{14,22},{16,8},{18,10},{20,12},{22,14},{9,1... | collective-permute-start | bytes 1572872 | tf_op jit(solution)/shard_map/ppermute | solution.py:402
  125.2 49.6 %collective-permute-start.14 = (bf16[256,1024]{1,0:T(8,128)(2,1)S(1)}, bf16[256,1024]{1,0:T(8,128)(2,1)S(1)}, u32[]{:S(2)}, u32[]{:S(2)}) collective-permute-start(bf16[256,1024]{1,0:T(8,128)(2,1)S(1)} %broadcast_select_fusion.3.refs_4_.refs_7_), channel_id=1, source_target_pairs={{0,2},{2,0},{4,6},{6,4},{8,10},{10,8},{12,14},{14,12},{16,18},{18,... | collective-permute-start | bytes 1572872 | tf_op jit(solution)/shard_map/ppermute | solution.py:402
  126.7 22.1 %copy-start.4 = (bf16[256,1024]{1,0:T(8,128)(2,1)S(1)}, bf16[256,1024]{1,0:T(8,128)(2,1)}, u32[]{:S(2)}) copy-start(bf16[256,1024]{1,0:T(8,128)(2,1)} %copy-done.3) | copy-start | bytes 1572868
  148.9 3.9 %copy-start.10 = (bf16[256,1024]{1,0:T(8,128)(2,1)}, bf16[256,1024]{1,0:T(8,128)(2,1)S(1)}, u32[]{:S(2)}) copy-start(bf16[256,1024]{1,0:T(8,128)(2,1)S(1)} %collective-permute-done.16.refs_2_.refs_5_) | copy-start | bytes 1572868
  148.9 25.9 %collective-permute-start.15 = (bf16[256,1024]{1,0:T(8,128)(2,1)S(1)}, bf16[256,1024]{1,0:T(8,128)(2,1)S(1)}, u32[]{:S(2)}, u32[]{:S(2)}) collective-permute-start(bf16[256,1024]{1,0:T(8,128)(2,1)S(1)} %copy-done.4), channel_id=1, source_target_pairs={{0,4},{2,6},{4,0},{6,2},{8,12},{10,14},{12,8},{14,10},{16,20},{18,... | collective-permute-start | bytes 1572872 | tf_op jit(solution)/shard_map/ppermute | solution.py:402
  150.3 2.4 %copy-start.13 = (bf16[256,1024]{1,0:T(8,128)(2,1)}, bf16[256,1024]{1,0:T(8,128)(2,1)S(1)}, u32[]{:S(2)}) copy-start(bf16[256,1024]{1,0:T(8,128)(2,1)S(1)} %collective-permute-done.17.refs_3_.refs_6_) | copy-start | bytes 1572868
  150.3 24.5 %collective-permute-start.20 = (bf16[256,1024]{1,0:T(8,128)(2,1)S(1)}, bf16[256,1024]{1,0:T(8,128)(2,1)S(1)}, u32[]{:S(2)}, u32[]{:S(2)}) collective-permute-start(bf16[256,1024]{1,0:T(8,128)(2,1)S(1)} %collective-permute-done.19), channel_id=1, source_target_pairs={{8,0},{10,2},{12,4},{14,6},{16,24},{18,26},{20,28},{22,30},{9,1},{... | collective-permute-start | bytes 1572872 | tf_op jit(solution)/shard_map/ppermute | solution.py:402
  174.8 1.2 copy-start.11

commit v2 on v1

v2 whole, which is shorter than its diff:
```python
import functools
import math

import jax
import jax.numpy as jnp
from jax import lax
from jax.experimental import pallas as pl
from jax.experimental.pallas import tpu as pltpu
from jax.sharding import PartitionSpec as P

HD = 128
PAGE = 16
CAP = 2
CUT = 1024
NORM_EPSILON = 1e-05
ROPE_THETA = 500000.0
LOW = -1e30
EXP2_SCALE = math.log2(math.e) / math.sqrt(HD)
VMEM_BYTES = 32 * 1024 * 1024
NT = (((1,), (1,)), ((), ()))


def params(limit=VMEM_BYTES):
    return pltpu.CompilerParams(vmem_limit_bytes=limit)


def stage_kernel(n_arrays, *refs):
    copies = [
        pltpu.make_async_copy(refs[i], refs[n_arrays + i], refs[2 * n_arrays].at[i])
        for i in range(n_arrays)
    ]
    for copy in copies:
        copy.start()
    for copy in copies:
        copy.wait()


def stage(*arrays):
    return pl.pallas_call(
        functools.partial(stage_kernel, len(arrays)),
        out_shape=tuple(jax.ShapeDtypeStruct(a.shape, a.dtype) for a in arrays),
        in_specs=[pl.BlockSpec(memory_space=pl.ANY)] * len(arrays),
        out_specs=[pl.BlockSpec(memory_space=pltpu.VMEM)] * len(arrays),
        scratch_shapes=[pltpu.SemaphoreType.DMA((len(arrays),))],
        compiler_params=params(),
        cost_estimate=pl.CostEstimate(
            flops=0, bytes_accessed=sum(2 * a.size * a.dtype.itemsize for a in arrays), transcendentals=0
        ),
        name="stage",
    )(*arrays)


def project_kernel(n_parts, chunk, order_ref, *refs):
    parts = refs[:n_parts]
    gain_ref, key_ref, value_ref, cos_ref, sin_ref, code_ref, out_ref, total_ref = refs[n_parts:]
    rows, part_width = parts[0].shape
    key_width = key_ref.shape[1]
    codes = code_ref[...]
    out_ref[rows:] = jnp.broadcast_to(codes, (codes.shape[0], 2 * key_width)).astype(jnp.bfloat16)
    squares = jnp.zeros((rows, HD), jnp.float32)
    for part in parts:
        for first in range(0, part_width, HD):
            piece = part[:, first : first + HD].astype(jnp.float32)
            squares += piece * piece
    squares = jnp.sum(squares, axis=1, keepdims=True)
    inverse = lax.rsqrt(squares * (1.0 / (part_width * n_parts)) + NORM_EPSILON)
    for index, part in enumerate(parts):
        base = order_ref[index] * part_width
        for first in range(0, part_width, chunk):
            where = pl.multiple_of(base + first, chunk)
            piece = part[:, first : first + chunk].astype(jnp.float32)
            normed = (piece * inverse * gain_ref[:, pl.ds(where, chunk)]).astype(jnp.bfloat16)
            keys = jnp.dot(
                normed, key_ref[pl.ds(where, chunk)], preferred_element_type=jnp.float32
            )
            values = jnp.dot(
                normed, value_ref[pl.ds(where, chunk)], preferred_element_type=jnp.float32
            )
            if index == 0 and first == 0:
                total_ref[:, :key_width] = keys
                total_ref[:, key_width:] = values
            else:
                total_ref[:, :key_width] += keys
                total_ref[:, key_width:] += values
    for head in range(key_width // HD):
        cut = slice(head * HD, (head + 1) * HD)
        raw = total_ref[:, cut]
        turned = raw * cos_ref[...] + pltpu.roll(raw, HD // 2, 1) * sin_ref[...]
        out_ref[:rows, cut] = turned.astype(jnp.bfloat16)
    out_ref[:rows, key_width:] = total_ref[:, key_width:].astype(jnp.bfloat16)


def project(parts, order, norm_gain, key_weight, value_weight, cosine, sine, codes):
    rows, part_width = parts[0].shape
    n_parts = len(parts)
    key_width = key_weight.shape[1]
    vmem = pl.BlockSpec(memory_space=pltpu.VMEM)
    return pl.pallas_call(
        functools.partial(project_kernel, n_parts, math.gcd(part_width, 1024)),
        out_shape=jax.ShapeDtypeStruct((rows + codes.shape[0], 2 * key_width), jnp.bfloat16),
        in_specs=[pl.BlockSpec(memory_space=pltpu.SMEM)] + [vmem] * (n_parts + 6),
        out_specs=vmem,
        scratch_shapes=[pltpu.VMEM((rows, 2 * key_width), jnp.float32)],
        compiler_params=params(),
        cost_estimate=pl.CostEstimate(
            flops=4 * rows * key_width * part_width * n_parts,
            bytes_accessed=4 * key_width * part_width * n_parts,
            transcendentals=0,
        ),
        name="project",
    )(order, *parts, norm_gain.reshape(1, -1), key_weight, value_weight, cosine, sine, codes)


def stack_heads(ref, group):
    return jnp.concatenate([ref[:, h * HD : (h + 1) * HD] for h in range(group)], axis=0)


def turned_with_ones(values):
    turned = values.T
    return jnp.concatenate([turned, jnp.ones((16, turned.shape[1]), turned.dtype)], axis=0)


def counted_piece(queries, keys, values_ones, counts, old_max):
    scores = lax.dot_general(keys, queries, NT, preferred_element_type=jnp.float32)
    scores = jnp.where(counts > 0, scores * EXP2_SCALE, LOW)
    new_max = jnp.maximum(old_max, jnp.max(scores, axis=0, keepdims=True))
    weights = jnp.where(counts > 0, jnp.exp2(scores - new_max) * counts, 0.0)
    product = jnp.dot(
        values_ones, weights.astype(jnp.bfloat16), preferred_element_type=jnp.float32
    )
    return new_max, product


def store_stats(stat_ref, columns, row_max, row_sum):
    stat_ref[0, 0:1, columns] = row_max
    stat_ref[0, 1:2, columns] = row_sum


def page_counts(ids, table_ref, length, store):
    pages, lanes = ids.shape
    found = jnp.zeros((pages, lanes), jnp.int32)
    for entry in range(table_ref.shape[0]):
        left = length - entry * PAGE
        weight = jnp.where(left >= PAGE, 1, jnp.where(left > 0, CUT, 0))
        found += jnp.where(ids == table_ref[entry : entry + 1, :], weight, 0)
    whole = (found & (CUT - 1)).astype(jnp.float32)
    cut = (found // CUT).astype(jnp.float32)
    token = lax.broadcasted_iota(jnp.int32, (PAGE, lanes), 0)
    kept = (token < length % PAGE).astype(jnp.float32)
    for page in range(pages):
        one = slice(page, page + 1)
        store(page, (whole[one] + cut[one] * kept).astype(jnp.bfloat16))


def resident_kernel(
    group, query_ref, key_ref, value_ref, table_ref, length_ref, acc_ref, stat_ref, counts
):
    queries = stack_heads(query_ref, group)
    rows = queries.shape[0]
    pages = counts.shape[0] // PAGE

    @pl.when(pl.program_id(0) == 0)
    def _():
        def store(page, found):
            counts[page * PAGE : (page + 1) * PAGE] = found

        ids = lax.broadcasted_iota(jnp.int32, (pages, rows), 0)
        page_counts(ids, table_ref, length_ref[...], store)

    new_max, product = counted_piece(
        queries,
        key_ref[...],
        turned_with_ones(value_ref[...]),
        counts[...].astype(jnp.float32),
        jnp.full((1, rows), LOW, jnp.float32),
    )
    acc_ref[0] = product[:HD]
    store_stats(stat_ref, slice(0, rows), new_max, product[HD : HD + 1])


def resident_attention(decode_query, keys, values, table, lengths):
    rows, query_width = decode_query.shape
    pool_rows, key_width = keys.shape
    kv_heads = key_width // HD
    group = query_width // key_width
    entries, lanes = table.shape
    return pl.pallas_call(
        functools.partial(resident_kernel, group),
        out_shape=(
            jax.ShapeDtypeStruct((kv_heads, HD, lanes), jnp.float32),
            jax.ShapeDtypeStruct((kv_heads, 8, lanes), jnp.float32),
        ),
        grid=(kv_heads,),
        in_specs=[
            pl.BlockSpec((rows, group * HD), lambda g: (0, g)),
            pl.BlockSpec((pool_rows, HD), lambda g: (0, g)),
            pl.BlockSpec((pool_rows, HD), lambda g: (0, g)),
            pl.BlockSpec((entries, lanes), lambda g: (0, 0)),
            pl.BlockSpec((1, lanes), lambda g: (0, 0)),
        ],
        out_specs=[
            pl.BlockSpec((1, HD, lanes), lambda g: (g, 0, 0)),
            pl.BlockSpec((1, 8, lanes), lambda g: (g, 0, 0)),
        ],
        scratch_shapes=[pltpu.VMEM((pool_rows, lanes), jnp.bfloat16)],
        compiler_params=params(60 * 2**20),
        cost_estimate=pl.CostEstimate(
            flops=6 * kv_heads * lanes * pool_rows * HD,
            bytes_accessed=4 * key_width * pool_rows,
            transcendentals=kv_heads * lanes * pool_rows,
        ),
        name="resident",
    )(decode_query, keys, values, table, lengths)


def attend_kernel(n_blocks, group, tile_heads, pool, first, final, place_ref, *refs):
    refs = list(refs)

    def take(count):
        taken, refs[:count] = refs[:count], []
        return taken

    query_ref, decode_ref = take(2)
    keys = take(n_blocks)
    values = take(n_blocks)
    codes = take(n_blocks)
    table_ref, length_ref = take(2)
    if not first:
        acc_in, stat_in = take(2)
    if final:
        side_acc, side_stat = take(2)
        out_ref, decode_out = take(2)
    else:
        acc_out, stat_out = take(2)
    (counts,) = refs
    rows = query_ref.shape[0]
    decode_rows = decode_ref.shape[0]
    own = place_ref[0]

    @pl.when(pl.program_id(0) == 0)
    def _():
        for b in range(n_blocks):
            section = place_ref[1 + b]
            slot = codes[b][...].astype(jnp.float32).astype(jnp.int32) - own * CAP
            mine = (slot >= 0) & (slot < CAP)
            if not (first and b == 0):
                mine &= section != own
            ids = jnp.where(mine, pool + section * CAP + slot, -1)

            def store(page, found, b=b):
                top = b * rows + page * PAGE
                counts[top : top + PAGE] = found

            page_counts(ids, table_ref, length_ref[...], store)

    all_keys = jnp.concatenate([ref[...] for ref in keys], axis=0)
    all_values = turned_with_ones(jnp.concatenate([ref[...] for ref in values], axis=0))
    seen = [place_ref[1 + b] < own for b in range(n_blocks)]
    tile = tile_heads * rows
    for top in range(0, group * rows, tile):
        here = slice(top, top + tile)
        heads = range(top // rows, top // rows + tile_heads)
        queries = jnp.concatenate([query_ref[:, h * HD : (h + 1) * HD] for h in heads], axis=0)
        scores = lax.dot_general(all_keys, queries, NT, preferred_element_type=jnp.float32)
        span = scores.shape[0] // n_blocks
        pieces = [scores[b * span : (b + 1) * span] for b in range(n_blocks)]
        if first:
            key_of = lax.broadcasted_iota(jnp.int32, (span, rows), 0)
            row_of = lax.broadcasted_iota(jnp.int32, (span, rows), 1)
            kept = jnp.concatenate([key_of <= row_of] * tile_heads, axis=1)
            pieces[0] = jnp.where(kept, pieces[0], LOW)
            new_max = jnp.max(pieces[0], axis=0, keepdims=True) * EXP2_SCALE
        else:
            old_max = stat_in[0, 0:1, here]
            new_max = old_max
        for b in range(1 if first else 0, n_blocks):
            highest = jnp.max(pieces[b], axis=0, keepdims=True) * EXP2_SCALE
            new_max = jnp.maximum(new_max, jnp.where(seen[b], highest, LOW))
        weights = []
        for b in range(n_blocks):
            shift = new_max
            if not (first and b == 0):
                shift = new_max + jnp.where(seen[b], 0.0, -LOW)
            weights.append(jnp.exp2(pieces[b] * EXP2_SCALE - shift).astype(jnp.bfloat16))
        product = jnp.dot(
            all_values, jnp.concatenate(weights, axis=0), preferred_element_type=jnp.float32
        )
        acc, total = product[:HD], product[HD : HD + 1]
        if not first:
            fade = jnp.exp2(old_max - new_max)
            acc += acc_in[0, :, here] * fade
            total += stat_in[0, 1:2, here] * fade
        if final:
            result = (acc / total).T.astype(jnp.bfloat16)
            for place, h in enumerate(heads):
                out_ref[:, h * HD : (h + 1) * HD] = result[place * rows : (place + 1) * rows]
        else:
            acc_out[0, :, here] = acc
            store_stats(stat_out, here, new_max, total)

    queries = stack_heads(decode_ref, group)
    small = group * decode_rows
    here = slice(group * rows, group * rows + small)
    if first:
        old_max = jnp.full((1, small), LOW, jnp.float32)
    else:
        old_max = stat_in[0, 0:1, here]
    new_max, product = counted_piece(
        queries,
        all_keys,
        all_values,
        counts[...].astype(jnp.float32),
        old_max,
    )
    acc, total = product[:HD], product[HD : HD + 1]
    if not first:
        fade = jnp.exp2(old_max - new_max)
        acc += acc_in[0, :, here] * fade
        total += stat_in[0, 1:2, here] * fade
    if final:
        side_max = side_stat[0, 0:1]
        top_max = jnp.maximum(new_max, side_max)
        fade, side_fade = jnp.exp2(new_max - top_max), jnp.exp2(side_max - top_max)
        acc = acc * fade + side_acc[0] * side_fade
        total = total * fade + side_stat[0, 1:2] * side_fade
        result = (acc / total).T.astype(jnp.bfloat16)
        for h in range(group):
            decode_out[:, h * HD : (h + 1) * HD] = result[h * decode_rows : (h + 1) * decode_rows]
    else:
        acc_out[0, :, here] = acc
        store_stats(stat_out, here, new_max, total)


def attend(place, query, decode_query, blocks, table, lengths, pool, state, side, kv_heads):
    n_blocks = len(blocks)
    rows, query_width = query.shape
    decode_rows = decode_query.shape[0]
    block_rows = rows
    pages = blocks[0].shape[0] - rows
    group = query_width // (kv_heads * HD)
    first, final = state is None, side is not None
    total_rows = group * (rows + decode_rows)
    small = group * decode_rows

    def by_head(*shape):
        return pl.BlockSpec((1, *shape), lambda g, place_ref: (g, 0, 0))

    query_spec = pl.BlockSpec((rows, group * HD), lambda g, place_ref: (0, g))
    decode_spec = pl.BlockSpec((decode_rows, group * HD), lambda g, place_ref: (0, g))
    key_spec = pl.BlockSpec((block_rows, HD), lambda g, place_ref: (0, g))
    value_spec = pl.BlockSpec((block_rows, HD), lambda g, place_ref: (0, kv_heads + g))
    code_spec = pl.BlockSpec((pages, small), lambda g, place_ref: (rows // pages, 0))
    operands = [query, decode_query, *blocks, *blocks, *blocks, table, lengths]
    in_specs = [query_spec, decode_spec] + [key_spec] * n_blocks + [value_spec] * n_blocks
    in_specs += [code_spec] * n_blocks
    in_specs += [
        pl.BlockSpec(table.shape, lambda g, place_ref: (0, 0)),
        pl.BlockSpec(lengths.shape, lambda g, place_ref: (0, 0)),
    ]
    if not first:
        operands += list(state)
        in_specs += [by_head(HD, total_rows), by_head(8, total_rows)]
    if final:
        operands += list(side)
        in_specs += [by_head(HD, small), by_head(8, small)]
        out_shape = (
            jax.ShapeDtypeStruct(query.shape, jnp.bfloat16),
            jax.ShapeDtypeStruct(decode_query.shape, jnp.bfloat16),
        )
        out_specs = [query_spec, decode_spec]
    else:
        out_shape = (
            jax.ShapeDtypeStruct((kv_heads, HD, total_rows), jnp.float32),
            jax.ShapeDtypeStruct((kv_heads, 8, total_rows), jnp.float32),
        )
        out_specs = [by_head(HD, total_rows), by_head(8, total_rows)]
    tile_heads = group
    pairs = kv_heads * total_rows * n_blocks * block_rows
    return pl.pallas_call(
        functools.partial(attend_kernel, n_blocks, group, tile_heads, pool, first, final),
        out_shape=out_shape,
        grid_spec=pltpu.PrefetchScalarGridSpec(
            num_scalar_prefetch=1,
            grid=(kv_heads,),
            in_specs=in_specs,
            out_specs=out_specs,
            scratch_shapes=[pltpu.VMEM((n_blocks * rows, small), jnp.bfloat16)],
        ),
        compiler_params=params(),
        cost_estimate=pl.CostEstimate(
            flops=6 * pairs * HD,
            bytes_accessed=12 * kv_heads * total_rows * HD,
            transcendentals=pairs,
        ),
        name="attend",
    )(place, *operands)


def page_codes(page_owner):
    page_index = jnp.arange(page_owner.shape[0], dtype=jnp.int32)
    earlier = (page_owner[:, None] == page_owner[None, :]) & (
        page_index[None, :] < page_index[:, None]
    )
    return (page_owner * CAP + jnp.sum(earlier.astype(jnp.int32), axis=1)).astype(jnp.float32)


def fence(*arrays):
    return lax.optimization_barrier(arrays)


def gather_rounds(own, work):
    def settle(moved, work):
        return fence(*moved, *work)[: len(moved)]

    size_z, size_y, size_x = 4, 2, 2
    here = lax.axis_index("section")
    z, column = here // 4, here % 4

    def index(zz, yy, xx):
        return (zz * size_y + yy) * size_x + xx

    def along_z(pairs):
        return [
            (index(a, yy, xx), index(b, yy, xx))
            for a, b in pairs
            for yy in range(size_y)
            for xx in range(size_x)
        ]

    every = [(zz, yy, xx) for zz in range(size_z) for yy in range(size_y) for xx in range(size_x)]
    swap_x = [(index(zz, yy, xx), index(zz, yy, 1 - xx)) for zz, yy, xx in every]
    swap_y = [(index(zz, yy, xx), index(zz, 1 - yy, xx)) for zz, yy, xx in every]
    ends = along_z([(0, 1), (1, 0), (2, 3), (3, 2)])
    middle = along_z([(1, 2), (2, 1)])
    outward = along_z([(1, 0), (2, 3)])
    inner = (z == 1) | (z == 2)

    def move(block, pairs):
        return lax.ppermute(block, "section", pairs)

    plane_a = jnp.bitwise_xor(z, 1)
    plane_f = jnp.where(inner, 3 - z, jnp.where(z == 0, 2, 1))
    plane_g = jnp.where(inner, jnp.bitwise_xor(3 - z, 1), 3 - z)

    def at(plane, turn):
        return plane * 4 + jnp.bitwise_xor(column, turn)

    moved = move(own, swap_x), move(own, swap_y), move(own, ends), move(own, middle)
    own_x, own_y, a, b = settle(moved, work)
    work = yield [(own, here), (own_x, at(z, 1)), (own_y, at(z, 2)), (a, at(plane_a, 0))]
    moved = move(own_y, swap_x), move(a, swap_y), move(b, outward), move(a, middle)
    own_d, a_y, c, d = settle(moved, work)
    f = jnp.where(inner, b, c)
    work = yield [(own_d, at(z, 3)), (a_y, at(plane_a, 2)), (f, at(plane_f, 0))]
    either = jnp.where(inner, d, own_d)
    moved = move(a, swap_x), move(f, swap_y), move(either, ends), move(own_d, middle)
    a_x, f_y, e, b_in = settle(moved, work)
    g = jnp.where(inner, d, e)
    work = yield [(a_x, at(plane_a, 1)), (f_y, at(plane_f, 2)), (g, at(plane_g, 0))]
    moved = move(f, swap_x), move(g, swap_y), move(b_in, outward), move(e, middle)
    f_x, g_y, c_in, d_in = settle(moved, work)
    f_d = jnp.where(inner, b_in, c_in)
    work = yield [(f_x, at(plane_f, 1)), (g_y, at(plane_g, 2)), (f_d, at(plane_f, 3))]
    moved = move(g, swap_x), move(a_x, swap_y), move(d_in, outward)
    g_x, a_turn, e_in = settle(moved, work)
    a_d = jnp.where(inner, e, a_turn)
    g_d = jnp.where(inner, d_in, e_in)
    yield [(g_x, at(plane_g, 1)), (a_d, at(plane_a, 3)), (g_d, at(plane_g, 3))]


def gather_plain(own, section_count):
    rows = own.shape[0]
    gathered = lax.all_gather(own, "section", axis=0, tiled=True)
    step = math.gcd(section_count, 4)
    for top in range(0, section_count, step):
        yield [
            (gathered[s * rows : (s + 1) * rows], jnp.int32(s)) for s in range(top, top + step)
        ]


def per_device(
    prefill_hidden,
    norm_gain,
    key_weight,
    value_weight,
    prefill_query,
    resident_keys,
    resident_values,
    decode_query,
    page_owner,
    block_table,
    context_len,
):
    section_count = lax.axis_size("section")
    tp_count = lax.axis_size("tp")
    section = lax.axis_index("section").astype(jnp.int32)
    tp = lax.axis_index("tp").astype(jnp.int32)
    rows = prefill_hidden.shape[0]
    key_width = key_weight.shape[1]
    kv_heads = key_width // HD
    group = prefill_query.shape[1] // key_width
    pool = resident_keys.shape[0]

    if tp_count == 2:
        other = lax.ppermute(prefill_hidden, "tp", [(0, 1), (1, 0)])
        parts, order = [prefill_hidden, other], jnp.stack([tp, 1 - tp])
    else:
        parts = [lax.all_gather(prefill_hidden, "tp", axis=1, tiled=True)]
        order = jnp.zeros((1,), jnp.int32)
    half = HD // 2
    frequency = jnp.exp(jnp.arange(half, dtype=jnp.float32) * (-2.0 * math.log(ROPE_THETA) / HD))
    positions = section * rows + jnp.arange(rows, dtype=jnp.int32)
    angles = positions.astype(jnp.float32)[:, None] * frequency[None, :]
    cosine, sine = jnp.cos(angles), jnp.sin(angles)
    cosine = jnp.concatenate([cosine, cosine], axis=1)
    sine = jnp.concatenate([-sine, sine], axis=1)

    key_near, value_near = stage(key_weight, value_weight)
    own = project(
        parts,
        order,
        norm_gain,
        key_near,
        value_near,
        cosine,
        sine,
        page_codes(page_owner).reshape(-1, 1),
    )

    own, block_table, context_len = fence(own, block_table, context_len)
    table = jnp.concatenate([block_table] * group, axis=0).T
    lengths = jnp.concatenate([context_len] * group)[None, :]
    side = resident_attention(
        decode_query,
        resident_keys.reshape(pool * PAGE, key_width),
        resident_values.reshape(pool * PAGE, key_width),
        table,
        lengths,
    )

    def step(arrived, state, side):
        place = jnp.stack([section] + [s.astype(jnp.int32) for _, s in arrived])
        blocks = [block for block, _ in arrived]
        return attend(
            place, prefill_query, decode_query, blocks, table, lengths, pool, state, side, kv_heads
        )

    if section_count == 16:
        rounds = gather_rounds(own, side)
        arrived, state = next(rounds), None
        for _ in range(4):
            state = step(arrived, state, None)
            arrived = rounds.send(state)
        return step(arrived, state, side)
    state = step([(own, section)], None, None)
    rounds = list(gather_plain(own, section_count))
    for arrived in rounds[:-1]:
        state = step(arrived, state, None)
    return step(rounds[-1], state, side)


def solution(mesh):
    return jax.shard_map(
        per_device,
        mesh=mesh,
        in_specs=(
            P("section", "tp"),
            P(),
            P(None, "tp"),
            P(None, "tp"),
            P("section", "tp"),
            P("section", None, "tp"),
            P("section", None, "tp"),
            P("section", "tp"),
            P("section"),
            P("section", None),
            P("section"),
        ),
        out_specs=(P("section", "tp"), P("section", "tp")),
        check_vma=False,
    )
```

time: 198 us -> 139 us (0.70); the launches traced: 196 us -> 139 us
  Pallas kernels: 126 us -> 95.7 us
  other arithmetic: 13.1 us -> 2.95 us
  waiting for transfers between devices: 15.1 us -> 5.87 us
  starting transfers between devices: 34.2 us -> 29.9 us
  matrix products: 2.02 us -> 0 us
    pallas_call x5, Pallas kernels: 102 us -> 73.3 us  [attend(): pl.pallas_call(functools.partial(attend_kernel, n_blocks, group, tile_hea...]
    ppermute x20 -> x19, waiting for transfers between devices: 15.1 us -> 5.86 us  [move(): return lax.ppermute(block, 'section', pairs)]
    all_to_all x1 -> x0, starting transfers between devices: 7.88 us -> none  [incoming_pages(): lax.all_to_all(sent, 'section', split_axis=0, concat_axis=0, tiled=True)]
    ppermute x20 -> x19, starting transfers between devices: 25.8 us -> 29.4 us  [move(): return lax.ppermute(block, 'section', pairs)]
    dot_general x4 -> x0, matrix products: 2.02 us -> none  [the longest x2 1.62 us: token_counts(): tokens = jnp.dot(stacked, spread, preferred_element_type=jnp.float32)]
    pallas_call x2 -> x3, Pallas kernels: 23.6 us -> 22.4 us  [the longest x1 10.5 us: resident_attention(): pl.pallas_call(functools.partial(resident_kernel, group), out_shape=(jax....]
  transfers between devices with their start and end apart: 22 -> 20, of which waited for: 4 -> 1; matrix products, arithmetic and copies ran while one was open for 9% -> 3% of each run, Pallas kernels for 47% -> 53%
where the time goes in v2:
time: 139 us
  Pallas kernels  95.7 us (69%)
  starting transfers between devices  29.9 us (22%)
  waiting for transfers between devices  5.87 us (4%)
  local copies, waits for them, and re-layouts  3.25 us (2%)
  other arithmetic  2.95 us (2%)
    pallas_call x5, Pallas kernels, attend(): pl.pallas_call(functools.partial(attend_kernel, n_blocks, group, tile_hea...  73.3 us
    ppermute x19, starting transfers between devices, move(): return lax.ppermute(block, 'section', pairs)  29.4 us
    pallas_call x1, Pallas kernels, resident_attention(): pl.pallas_call(functools.partial(resident_kernel, group), out_shape=(jax....  10.5 us
    pallas_call x1, Pallas kernels, project(): pl.pallas_call(functools.partial(project_kernel, n_parts, math.gcd(part_w...  5.95 us
    pallas_call x1, Pallas kernels, stage(): pl.pallas_call(functools.partial(stage_kernel, len(arrays)), out_shape=tu...  5.93 us
    ppermute x19, waiting for transfers between devices, move(): return lax.ppermute(block, 'section', pairs)  5.86 us
  transfers between devices with their start and end apart: 20, of which 1 were waited for; matrix products, arithmetic and copies ran while one was open for 3% of the time, Pallas kernels for 53%

profile of v2, /device:TPU:0, one launch (start us, length us, event | category | flops | bytes accessed | tf_op | source)
XLA Modules:
  0.0 138.8 jit_solution(10586336495094810118)
XLA Ops:
  0.6 0.5 collective-permute-start
  1.1 0.9 convert_reduce_fusion
  2.1 0.7 convert_bitcast_fusion
  2.7 0.1 copy.22.refs_7_
  2.8 5.9 %stage.1 = (bf16[8192,512]{1,0:T(8,128)(2,1)S(1)}, bf16[8192,512]{1,0:T(8,128)(2,1)S(1)}) custom-call(bf16[8192,512]{1,0:T(8,128)(2,1)} %refs_0_.7, bf16[8192,512]{1,0:T(8,128)(2,1)} %refs_1_.6), custom_call_target="tpu_custom_call" | custom-call | bytes 33554432 | tf_op jit(solution)/shard_map/stage/pallas_call | solution.py:39
  8.8 0.1 pad_add_fusion.1.order_ref
  8.9 0.5 fusion
  9.4 0.1 pad_maximum_fusion
  9.6 5.9 %project.1.refs_2_.refs_6_.refs_10_ = bf16[272,1024]{1,0:T(8,128)(2,1)S(1)} custom-call(s32[2]{0:T(128)S(1)} %pad_add_fusion.1.order_ref, bf16[256,4096]{1,0:T(8,128)(2,1)S(1)} %copy-done, bf16[256,4096]{1,0:T(8,128)(2,1)S(1)} %collective-permute-done.refs_1_, f32[1,8192]{1,0:T(1,128)S(1)} %bitcast.31, bf16[8192,512]{1,0:T(8,128)(2,1)S(1)} %get-tuple-element.36.refs_3_, ...), custom_call_target="tpu_custom_call" | custom-call | flops 4294967296 | bytes 16777216 | tf_op jit(solution)/shard_map/project/pallas_call | solution.py:98
  15.5 2.6 %collective-permute-start.1 = (bf16[272,1024]{1,0:T(8,128)(2,1)S(1)}, bf16[272,1024]{1,0:T(8,128)(2,1)S(1)}, u32[]{:S(2)}, u32[]{:S(2)}) collective-permute-start(bf16[272,1024]{1,0:T(8,128)(2,1)S(1)} %project.1.refs_2_.refs_6_.refs_10_), channel_id=1, source_target_pairs={{0,2},{2,0},{4,6},{6,4},{8,10},{10,8},{12,14},{14,12},{16,18},{18,... | collective-permute-start | bytes 1671176 | tf_op jit(solution)/shard_map/ppermute | solution.py:439
  18.1 1.5 %collective-permute-start.2 = (bf16[272,1024]{1,0:T(8,128)(2,1)S(1)}, bf16[272,1024]{1,0:T(8,128)(2,1)S(1)}, u32[]{:S(2)}, u32[]{:S(2)}) collective-permute-start(bf16[272,1024]{1,0:T(8,128)(2,1)S(1)} %project.1.refs_2_.refs_6_.refs_10_), channel_id=1, source_target_pairs={{0,4},{2,6},{4,0},{6,2},{8,12},{10,14},{12,8},{14,10},{16,20},{18,... | collective-permute-start | bytes 1671176 | tf_op jit(solution)/shard_map/ppermute | solution.py:439
  19.6 1.6 %collective-permute-start.3 = (bf16[272,1024]{1,0:T(8,128)(2,1)S(1)}, bf16[272,1024]{1,0:T(8,128)(2,1)S(1)}, u32[]{:S(2)}, u32[]{:S(2)}) collective-permute-start(bf16[272,1024]{1,0:T(8,128)(2,1)S(1)} %project.1.refs_2_.refs_6_.refs_10_), channel_id=1, source_target_pairs={{0,8},{2,10},{4,12},{6,14},{8,0},{10,2},{12,4},{14,6},{16,24},{18,... | collective-permute-start | bytes 1671176 | tf_op jit(solution)/shard_map/ppermute | solution.py:439
  21.2 0.7 collective-permute-start.4
  22.0 0.1 stack.88.place_ref
  22.1 0.1 pad_add_fusion.2
  22.1 0.1 copy.23
  22.2 0.7 concatenate.14
  23.0 0.6 concatenate.15
  23.6 10.5 %resident.1 = (f32[4,128,128]{2,1,0:T(8,128)}, f32[4,8,128]{2,1,0:T(8,128)}) custom-call(bf16[16,4096]{1,0:T(8,128)(2,1)} %refs_1_.11, bf16[4096,512]{1,0:T(8,128)(2,1)} %bitcast.38, bf16[4096,512]{1,0:T(8,128)(2,1)} %bitcast.39, s32[62,128]{1,0:T(8,128)} %bitcast.25, s32[1,128]{1,0:T(1,128)} %bitcast.32), custom_call_target="tpu_custom_call" | custom-call | flops 1610612736 | bytes 8388608 | tf_op jit(solution)/shard_map/resident/pallas_call | solution.py:187
  34.1 0.6 collective-permute-start.6
  34.7 0.7 collective-permute-start.8
  35.4 0.6 collective-permute-start.9
  36.0 1.5 %collective-permute-start.5 = (bf16[272,1024]{1,0:T(8,128)(2,1)S(1)}, bf16[272,1024]{1,0:T(8,128)(2,1)S(1)}, u32[]{:S(2)}, u32[]{:S(2)}) collective-permute-start(bf16[272,1024]{1,0:T(8,128)(2,1)S(1)} %collective-permute-done.2.refs_4_.refs_8_.refs_12_), channel_id=1, source_target_pairs={{0,2},{2,0},{4,6},{6,4},{8,10},{10,8},{12,14},{14,12},{16,18},{18,... | collective-permute-start | bytes 1671176 | tf_op jit(solution)/shard_map/ppermute | solution.py:439
  37.5 1.5 %collective-permute-start.7 = (bf16[272,1024]{1,0:T(8,128)(2,1)S(1)}, bf16[272,1024]{1,0:T(8,128)(2,1)S(1)}, u32[]{:S(2)}, u32[]{:S(2)}) collective-permute-start(bf16[272,1024]{1,0:T(8,128)(2,1)S(1)} %collective-permute-done.4), channel_id=1, source_target_pairs={{8,0},{10,2},{12,4},{14,6},{16,24},{18,26},{20,28},{22,30},{9,1},{... | collective-permute-start | bytes 1671176 | tf_op jit(solution)/shard_map/ppermute | solution.py:439
  39.0 1.6 %copy-done.5 = bf16[256,4096]{1,0:T(8,128)(2,1)S(1)} copy-done((bf16[256,4096]{1,0:T(8,128)(2,1)S(1)}, bf16[256,4096]{1,0:T(8,128)(2,1)}, u32[]{:S(2)}) %copy-start.5) | copy-done | bytes 2097176
  40.6 14.9 %attend.5 = (f32[4,128,2176]{2,1,0:T(8,128)S(1)}, f32[4,8,2176]{2,1,0:T(8,128)S(1)}) custom-call(s32[5]{0:T(128)S(1)} %stack.88.place_ref, bf16[256,4096]{1,0:T(8,128)(2,1)S(1)} %copy-done.5, bf16[16,4096]{1,0:T(8,128)(2,1)S(1)} %copy-done.1, bf16[272,1024]{1,0:T(8,128)(2,1)S(1)} %project.1.refs_2_.refs_6_.refs_10_, ...), custom_call_target="tpu_custom_call" | custom-call | flops 6845104128 | bytes 13369344 | tf_op jit(solution)/shard_map/attend/pallas_call | solution.py:379
  55.5 5.8 %collective-permute-done.5.refs_2_.refs_5_.refs_8_ = bf16[272,1024]{1,0:T(8,128)(2,1)S(1)} collective-permute-done((bf16[272,1024]{1,0:T(8,128)(2,1)S(1)}, bf16[272,1024]{1,0:T(8,128)(2,1)S(1)}, u32[]{:S(2)}, u32[]{:S(2)}) %collective-permute-start.5) | collective-permute-done | bytes 557088 | tf_op jit(solution)/shard_map/ppermute | solution.py:439
  61.3 0.1 broadcast_select_fusion.5.refs_4_.refs_7_.refs_10_
  61.4 0.7 collective-permute-start.12
  62.1 0.1 broadcast_select_fusion.4
  62.2 8.3 %collective-permute-start.11 = (bf16[272,1024]{1,0:T(8,128)(2,1)S(1)}, bf16[272,1024]{1,0:T(8,128)(2,1)S(1)}, u32[]{:S(2)}, u32[]{:S(2)}) collective-permute-start(bf16[272,1024]{1,0:T(8,128)(2,1)S(1)} %broadcast_select_fusion.4), channel_id=1, source_target_pairs={{0,8},{2,10},{4,12},{6,14},{8,0},{10,2},{12,4},{14,6},{16,24},{18,... | collective-permute-start | bytes 1671176 | tf_op jit(solution)/shard_map/ppermute | solution.py:439
  70.5 1.5 %collective-permute-start.10 = (bf16[272,1024]{1,0:T(8,128)(2,1)S(1)}, bf16[272,1024]{1,0:T(8,128)(2,1)S(1)}, u32[]{:S(2)}, u32[]{:S(2)}) collective-permute-start(bf16[272,1024]{1,0:T(8,128)(2,1)S(1)} %broadcast_select_fusion.5.refs_4_.refs_7_.refs_10_), channel_id=1, source_target_pairs={{0,4},{2,6},{4,0},{6,2},{8,12},{10,14},{12,8},{14,10},{16,20},{18,... | collective-permute-start | bytes 1671176 | tf_op jit(solution)/shard_map/ppermute | solution.py:439
  72.0 0.1 pad_add_fusion.4.place_ref
  72.1 0.5 collective-permute-start.15
  72.6 14.2 %attend.6 = (f32[4,128,2176]{2,1,0:T(8,128)S(1)}, f32[4,8,2176]{2,1,0:T(8,128)S(1)}) custom-call(s32[4]{0:T(128)S(1)} %get-tuple-element.73.place_ref, bf16[256,4096]{1,0:T(8,128)(2,1)S(1)} %copy-done.5, bf16[16,4096]{1,0:T(8,128)(2,1)S(1)} %copy-done.1, bf16[272,1024]{1,0:T(8,128)(2,1)S(1)} %collective-permute-done.5.refs_2_.refs_5_.refs_8_, ...), custom_call_target="tpu_custom_call" | custom-call | flops 5133828096 | bytes 13369344 | tf_op jit(solution)/shard_map/attend/pallas_call | solution.py:379
  87.0 0.7 collective-permute-start.18
  87.7 0.6 collective-permute-start.16
  88.3 1.3 collective-permute-start.17
  89.6 0.1 pad_add_fusion.place_ref
  89.7 1.5 %collective-permute-start.13 = (bf16[272,1024]{1,0:T(8,128)(2,1)S(1)}, bf16[272,1024]{1,0:T(8,128)(2,1)S(1)}, u32[]{:S(2)}, u32[]{:S(2)}) collective-permute-start(bf16[272,1024]{1,0:T(8,128)(2,1)S(1)} %broadcast_select_fusion.3.refs_4_.refs_7_.refs_10_), channel_id=1, source_target_pairs={{0,2},{2,0},{4,6},{6,4},{8,10},{10,8},{12,14},{14,12},{16,18},{18,... | collective-permute-start | bytes 1671176 | tf_op jit(solution)/shard_map/ppermute | solution.py:439
  91.1 14.3 %attend.7 = (f32[4,128,2176]{2,1,0:T(8,128)S(1)}, f32[4,8,2176]{2,1,0:T(8,128)S(1)}) custom-call(s32[4]{0:T(128)S(1)} %get-tuple-element.74.place_ref, bf16[256,4096]{1,0:T(8,128)(2,1)S(1)} %copy-done.5, bf16[16,4096]{1,0:T(8,128)(2,1)S(1)} %copy-done.1, bf16[272,1024]{1,0:T(8,128)(2,1)S(1)} %collective-permute-done.9.refs_2_.refs_5_.refs_8_, ...), custom_call_target="tpu_custom_call" | custom-call | flops 5133828096 | bytes 13369344 | tf_op jit(solution)/shard_map/attend/pallas_call | solution.py:379
  105.4 1.6 %collective-permute-start.14 = (bf16[272,1024]{1,0:T(8,128)(2,1)S(1)}, bf16[272,1024]{1,0:T(8,128)(2,1)S(1)}, u32[]{:S(2)}, u32[]{:S(2)}) collective-permute-start(bf16[272,1024]{1,0:T(8,128)(2,1)S(1)} %collective-permute-done.9.refs_2_.refs_5_.refs_8_), channel_id=1, source_target_pairs={{0,4},{2,6},{4,0},{6,2},{8,12},{10,14},{12,8},{14,10},{16,20},{18,... | collective-permute-start | bytes 1671176 | tf_op jit(solution)/shard_map/ppermute | solution.py:439
  107.0 1.5 %collective-permute-start.19 = (bf16[272,1024]{1,0:T(8,128)(2,1)S(1)}, bf16[272,1024]{1,0:T(8,128)(2,1)S(1)}, u32[]{:S(2)}, u32[]{:S(2)}) collective-permute-start(bf16[272,1024]{1,0:T(8,128)(2,1)S(1)} %collective-permute-done.18), channel_id=1, source_target_pairs={{8,0},{10,2},{12,4},{14,6},{16,24},{18,26},{20,28},{22,30},{9,1},{... | collective-permute-start | bytes 1671176 | tf_op jit(solution)/shard_map/ppermute | solution.py:439
  108.6 0.1 broadcast_select_fusion.2.refs_4_.refs_7_.refs_10_
  108.6 14.3 %attend.8 = (f32[4,128,2176]{2,1,0:T(8,128)S(1)}, f32[4,8,2176]{2,1,0:T(8,128)S(1)}) custom-call(s32[4]{0:T(128)S(1)} %pad_add_fusion.4.place_ref, bf16[256,4096]{1,0:T(8,128)(2,1)S(1)} %copy-done.5, bf16[16,4096]{1,0:T(8,128)(2,1)S(1)} %copy-done.1, bf16[272,1024]{1,0:T(8,128)(2,1)S(1)} %collective-permute-done.15.refs_2_.refs_5_.refs_8_, ...), custom_call_target="tpu_custom_call" | custom-call | flops 5133828096 | bytes 13369344 | tf_op jit(solution)/shard_map/attend/pallas_call | solution.py:379
  123.0 0.1 broadcast_select_fusion.refs_4_.refs_7_.refs_10_
  123.1 0.1 broadcast_select_fusion.1.refs_3_.refs_6_.refs_9_
  123.2 15.6 %attend.9 = (bf16[256,4096]{1,0:T(8,128)(2,1)}, bf16[16,4096]{1,0:T(8,128)(2,1)}) custom-call(s32[4]{0:T(128)S(1)} %pad_add_fusion.place_ref, bf16[256,4096]{1,0:T(8,128)(2,1)S(1)} %copy-done.5, bf16[16,4096]{1,0:T(8,128)(2,1)S(1)} %copy-done.1, bf16[272,1024]{1,0:T(8,128)(2,1)S(1)} %collective-permute-done.13.refs_2_.refs_5_.refs_8_, ...), custom_call_target="tpu_custom_call" | custom-call | flops 5133828096 | bytes 13369344 | tf_op jit(solution)/shard_map/attend/pallas_call | solution.py:379
  (41 shorter events, 0.2 us)
Async XLA Ops:
  0.6 8.9 %collective-permute-start = (bf16[256,4096]{1,0:T(8,128)(2,1)}, bf16[256,4096]{1,0:T(8,128)(2,1)S(1)}, u32[]{:S(2)}, u32[]{:S(2)}) collective-permute-start(bf16[256,4096]{1,0:T(8,128)(2,1)} %refs_0_.8), channel_id=1, source_target_pairs={{0,1},{1,0},{2,3},{3,2},{4,5},{5,4},{6,7},{7,6},{8,9},{9,8},{10,11... | collective-permute-start | bytes 6291464 | tf_op jit(solution)/shard_map/ppermute | solution.py:505
  2.8 6.7 %copy-start = (bf16[256,4096]{1,0:T(8,128)(2,1)S(1)}, bf16[256,4096]{1,0:T(8,128)(2,1)}, u32[]{:S(2)}) copy-start(bf16[256,4096]{1,0:T(8,128)(2,1)} %refs_0_.8) | copy-start | bytes 6291460
  2.8 6.7 %copy-start.3 = (f32[8192]{0:T(1024)S(1)}, f32[8192]{0:T(1024)}, u32[]{:S(2)}) copy-start(f32[8192]{0:T(1024)} %param.12) | copy-start | bytes 98308
  9.6 12.6 %copy-start.9 = (s32[16,62]{1,0:T(8,128)S(1)}, s32[16,62]{1,0:T(8,128)}, u32[]{:S(2)}) copy-start(s32[16,62]{1,0:T(8,128)} %param.20) | copy-start | bytes 11908
  9.6 13.4 %copy-start.8 = (s32[16]{0:T(128)S(1)}, s32[16]{0:T(128)}, u32[]{:S(2)}) copy-start(s32[16]{0:T(128)} %param.21) | copy-start | bytes 196
  15.5 18.6 %collective-permute-start.1 = (bf16[272,1024]{1,0:T(8,128)(2,1)S(1)}, bf16[272,1024]{1,0:T(8,128)(2,1)S(1)}, u32[]{:S(2)}, u32[]{:S(2)}) collective-permute-start(bf16[272,1024]{1,0:T(8,128)(2,1)S(1)} %project.1.refs_2_.refs_6_.refs_10_), channel_id=1, source_target_pairs={{0,2},{2,0},{4,6},{6,4},{8,10},{10,8},{12,14},{14,12},{16,18},{18,... | collective-permute-start | bytes 1671176 | tf_op jit(solution)/shard_map/ppermute | solution.py:439
  18.1 16.0 %collective-permute-start.2 = (bf16[272,1024]{1,0:T(8,128)(2,1)S(1)}, bf16[272,1024]{1,0:T(8,128)(2,1)S(1)}, u32[]{:S(2)}, u32[]{:S(2)}) collective-permute-start(bf16[272,1024]{1,0:T(8,128)(2,1)S(1)} %project.1.refs_2_.refs_6_.refs_10_), channel_id=1, source_target_pairs={{0,4},{2,6},{4,0},{6,2},{8,12},{10,14},{12,8},{14,10},{16,20},{18,... | collective-permute-start | bytes 1671176 | tf_op jit(solution)/shard_map/ppermute | solution.py:439
  19.6 14.5 %collective-permute-start.3 = (bf16[272,1024]{1,0:T(8,128)(2,1)S(1)}, bf16[272,1024]{1,0:T(8,128)(2,1)S(1)}, u32[]{:S(2)}, u32[]{:S(2)}) collective-permute-start(bf16[272,1024]{1,0:T(8,128)(2,1)S(1)} %project.1.refs_2_.refs_6_.refs_10_), channel_id=1, source_target_pairs={{0,8},{2,10},{4,12},{6,14},{8,0},{10,2},{12,4},{14,6},{16,24},{18,... | collective-permute-start | bytes 1671176 | tf_op jit(solution)/shard_map/ppermute | solution.py:439
  21.2 12.9 %collective-permute-start.4 = (bf16[272,1024]{1,0:T(8,128)(2,1)S(1)}, bf16[272,1024]{1,0:T(8,128)(2,1)S(1)}, u32[]{:S(2)}, u32[]{:S(2)}) collective-permute-start(bf16[272,1024]{1,0:T(8,128)(2,1)S(1)} %project.1.refs_2_.refs_6_.refs_10_), channel_id=1, source_target_pairs={{8,16},{10,18},{12,20},{14,22},{16,8},{18,10},{20,12},{22,14},{9,1... | collective-permute-start | bytes 1671176 | tf_op jit(solution)/shard_map/ppermute | solution.py:439
  22.1 16.9 %copy-start.1 = (bf16[16,4096]{1,0:T(8,128)(2,1)S(1)}, bf16[16,4096]{1,0:T(8,128)(2,1)}, u32[]{:S(2)}) copy-start(bf16[16,4096]{1,0:T(8,128)(2,1)} %refs_1_.11) | copy-start | bytes 393220
  23.0 16.0 %copy-start.2 = (s32[128,62]{0,1:T(8,128)S(1)}, s32[128,62]{0,1:T(8,128)}, u32[]{:S(2)}) copy-start(s32[128,62]{0,1:T(8,128)} %concatenate.14) | copy-start | bytes 95236
  23.6 15.4 %copy-start.4 = (s32[128]{0:T(128)S(1)}, s32[128]{0:T(128)}, u32[]{:S(2)}) copy-start(s32[128]{0:T(128)} %concatenate.15) | copy-start | bytes 1540
  34.1 27.2 %collective-permute-start.6 = (bf16[272,1024]{1,0:T(8,128)(2,1)S(1)}, bf16[272,1024]{1,0:T(8,128)(2,1)S(1)}, u32[]{:S(2)}, u32[]{:S(2)}) collective-permute-start(bf16[272,1024]{1,0:T(8,128)(2,1)S(1)} %collective-permute-done.3.refs_5_.refs_9_.refs_13_), channel_id=1, source_target_pairs={{0,4},{2,6},{4,0},{6,2},{8,12},{10,14},{12,8},{14,10},{16,20},{18,... | collective-permute-start | bytes 1671176 | tf_op jit(solution)/shard_map/ppermute | solution.py:439
  34.7 26.6 %collective-permute-start.8 = (bf16[272,1024]{1,0:T(8,128)(2,1)S(1)}, bf16[272,1024]{1,0:T(8,128)(2,1)S(1)}, u32[]{:S(2)}, u32[]{:S(2)}) collective-permute-start(bf16[272,1024]{1,0:T(8,128)(2,1)S(1)} %collective-permute-done.3.refs_5_.refs_9_.refs_13_), channel_id=1, source_target_pairs={{8,16},{10,18},{12,20},{14,22},{16,8},{18,10},{20,12},{22,14},{9,1... | collective-permute-start | bytes 1671176 | tf_op jit(solution)/shard_map/ppermute | solution.py:439
  35.4 51.5 %collective-permute-start.9 = (bf16[272,1024]{1,0:T(8,128)(2,1)S(1)}, bf16[272,1024]{1,0:T(8,128)(2,1)S(1)}, u32[]{:S(2)}, u32[]{:S(2)}) collective-permute-start(bf16[272,1024]{1,0:T(8,128)(2,1)S(1)} %collective-permute-done.3.refs_5_.refs_9_.refs_13_), channel_id=1, source_target_pairs={{0,2},{2,0},{4,6},{6,4},{8,10},{10,8},{12,14},{14,12},{16,18},{18,... | collective-permute-start | bytes 1671176 | tf_op jit(solution)/shard_map/ppermute | solution.py:439
  36.0 25.3 %collective-permute-start.5 = (bf16[272,1024]{1,0:T(8,128)(2,1)S(1)}, bf16[272,1024]{1,0:T(8,128)(2,1)S(1)}, u32[]{:S(2)}, u32[]{:S(2)}) collective-permute-start(bf16[272,1024]{1,0:T(8,128)(2,1)S(1)} %collective-permute-done.2.refs_4_.refs_8_.refs_12_), channel_id=1, source_target_pairs={{0,2},{2,0},{4,6},{6,4},{8,10},{10,8},{12,14},{14,12},{16,18},{18,... | collective-permute-start | bytes 1671176 | tf_op jit(solution)/shard_map/ppermute | solution.py:439
  37.5 23.8 %collective-permute-start.7 = (bf16[272,1024]{1,0:T(8,128)(2,1)S(1)}, bf16[272,1024]{1,0:T(8,128)(2,1)S(1)}, u32[]{:S(2)}, u32[]{:S(2)}) collective-permute-start(bf16[272,1024]{1,0:T(8,128)(2,1)S(1)} %collective-permute-done.4), channel_id=1, source_target_pairs={{8,0},{10,2},{12,4},{14,6},{16,24},{18,26},{20,28},{22,30},{9,1},{... | collective-permute-start | bytes 1671176 | tf_op jit(solution)/shard_map/ppermute | solution.py:439
  39.0 1.6 %copy-start.5 = (bf16[256,4096]{1,0:T(8,128)(2,1)S(1)}, bf16[256,4096]{1,0:T(8,128)(2,1)}, u32[]{:S(2)}) copy-start(bf16[256,4096]{1,0:T(8,128)(2,1)} %refs_0_.13) | copy-start | bytes 6291460
  61.4 25.5 %collective-permute-start.12 = (bf16[272,1024]{1,0:T(8,128)(2,1)S(1)}, bf16[272,1024]{1,0:T(8,128)(2,1)S(1)}, u32[]{:S(2)}, u32[]{:S(2)}) collective-permute-start(bf16[272,1024]{1,0:T(8,128)(2,1)S(1)} %collective-permute-done.5.refs_2_.refs_5_.refs_8_), channel_id=1, source_target_pairs={{8,16},{10,18},{12,20},{14,22},{16,8},{18,10},{20,12},{22,14},{9,1... | collective-permute-start | bytes 1671176 | tf_op jit(solution)/shard_map/ppermute | solution.py:439
  62.2 24.7 %collective-permute-start.11 = (bf16[272,1024]{1,0:T(8,128)(2,1)S(1)}, bf16[272,1024]{1,0:T(8,128)(2,1)S(1)}, u32[]{:S(2)}, u32[]{:S(2)}) collective-permute-start(bf16[272,1024]{1,0:T(8,128)(2,1)S(1)} %broadcast_select_fusion.4), channel_id=1, source_target_pairs={{0,8},{2,10},{4,12},{6,14},{8,0},{10,2},{12,4},{14,6},{16,24},{18,... | collective-permute-start | bytes 1671176 | tf_op jit(solution)/shard_map/ppermute | solution.py:439
  70.5 16.4 %collective-permute-start.10 = (bf16[272,1024]{1,0:T(8,128)(2,1)S(1)}, bf16[272,1024]{1,0:T(8,128)(2,1)S(1)}, u32[]{:S(2)}, u32[]{:S(2)}) collective-permute-start(bf16[272,1024]{1,0:T(8,128)(2,1)S(1)} %broadcast_select_fusion.5.refs_4_.refs_7_.refs_10_), channel_id=1, source_target_pairs={{0,4},{2,6},{4,0},{6,2},{8,12},{10,14},{12,8},{14,10},{16,20},{18,... | collective-permute-start | bytes 1671176 | tf_op jit(solution)/shard_map/ppermute | solution.py:439
  72.1 33.3 %collective-permute-start.15 = (bf16[272,1024]{1,0:T(8,128)(2,1)S(1)}, bf16[272,1024]{1,0:T(8,128)(2,1)S(1)}, u32[]{:S(2)}, u32[]{:S(2)}) collective-permute-start(bf16[272,1024]{1,0:T(8,128)(2,1)S(1)} %broadcast_select_fusion.5.refs_4_.refs_7_.refs_10_), channel_id=1, source_target_pairs={{0,2},{2,0},{4,6},{6,4},{8,10},{10,8},{12,14},{14,12},{16,18},{18,... | collective-permute-start | bytes 1671176 | tf_op jit(solution)/shard_map/ppermute | solution.py:439
  87.0 20.0 %collective-permute-start.18 = (bf16[272,1024]{1,0:T(8,128)(2,1)S(1)}, bf16[272,1024]{1,0:T(8,128)(2,1)S(1)}, u32[]{:S(2)}, u32[]{:S(2)}) collective-permute-start(bf16[272,1024]{1,0:T(8,128)(2,1)S(1)} %collective-permute-done.11), channel_id=1, source_target_pairs={{8,16},{10,18},{12,20},{14,22},{16,8},{18,10},{20,12},{22,14},{9,1... | collective-permute-start | bytes 1671176 | tf_op jit(solution)/shard_map/ppermute | solution.py:439
  87.7 19.3 %collective-permute-start.16 = (bf16[272,1024]{1,0:T(8,128)(2,1)S(1)}, bf16[272,1024]{1,0:T(8,128)(2,1)S(1)}, u32[]{:S(2)}, u32[]{:S(2)}) collective-permute-start(bf16[272,1024]{1,0:T(8,128)(2,1)S(1)} %broadcast_select_fusion.3.refs_4_.refs_7_.refs_10_), channel_id=1, source_target_pairs={{0,4},{2,6},{4,0},{6,2},{8,12},{10,14},{12,8},{14,10},{16,20},{18,... | collective-permute-start | bytes 1671176 | tf_op jit(solution)/shard_map/ppermute | solution.py:439
  88.3 18.7 %collective-permute-start.17 = (bf16[272,1024]{1,0:T(8,128)(2,1)S(1)}, bf16[272,1024]{1,0:T(8,128)(2,1)S(1)}, u32[]{:S(2)}, u32[]{:S(2)}) collective-permute-start(bf16[272,1024]{1,0:T(8,128)(2,1)S(1)} %collective-permute-done.12), channel_id=1, source_target_pairs={{8,0},{10,2},{12,4},{14,6},{16,24},{18,26},{20,28},{22,30},{9,1},{... | collective-permute-start | bytes 1671176 | tf_op jit(solution)/shard_map/ppermute | solution.py:439
  89.7 33.3 %collective-permute-start.13 = (bf16[272,1024]{1,0:T(8,128)(2,1)S(1)}, bf16[272,1024]{1,0:T(8,128)(2,1)S(1)}, u32[]{:S(2)}, u32[]{:S(2)}) collective-permute-start(bf16[272,1024]{1,0:T(8,128)(2,1)S(1)} %broadcast_select_fusion.3.refs_4_.refs_7_.refs_10_), channel_id=1, source_target_pairs={{0,2},{2,0},{4,6},{6,4},{8,10},{10,8},{12,14},{14,12},{16,18},{18,... | collective-permute-start | bytes 1671176 | tf_op jit(solution)/shard_map/ppermute | solution.py:439
  105.4 17.5 %collective-permute-start.14 = (bf16[272,1024]{1,0:T(8,128)(2,1)S(1)}, bf16[272,1024]{1,0:T(8,128)(2,1)S(1)}, u32[]{:S(2)}, u32[]{:S(2)}) collective-permute-start(bf16[272,1024]{1,0:T(8,128)(2,1)S(1)} %collective-permute-done.9.refs_2_.refs_5_.refs_8_), channel_id=1, source_target_pairs={{0,4},{2,6},{4,0},{6,2},{8,12},{10,14},{12,8},{14,10},{16,20},{18,... | collective-permute-start | bytes 1671176 | tf_op jit(solution)/shard_map/ppermute | solution.py:439
  107.0 16.0 %collective-permute-start.19 = (bf16[272,1024]{1,0:T(8,128)(2,1)S(1)}, bf16[272,1024]{1,0:T(8,128)(2,1)S(1)}, u32[]{:S(2)}, u32[]{:S(2)}) collective-permute-start(bf16[272,1024]{1,0:T(8,128)(2,1)S(1)} %collective-permute-done.18), channel_id=1, source_target_pairs={{8,0},{10,2},{12,4},{14,6},{16,24},{18,26},{20,28},{22,30},{9,1},{... | collective-permute-start | bytes 1671176 | tf_op jit(solution)/shard_map/ppermute | solution.py:439
  108.6 14.5 %copy-start.6 = (f32[4,128,128]{2,1,0:T(8,128)S(1)}, f32[4,128,128]{2,1,0:T(8,128)}, u32[]{:S(2)}) copy-start(f32[4,128,128]{2,1,0:T(8,128)} %get-tuple-element.41.refs_15_) | copy-start | bytes 786436
  108.6 14.5 %copy-start.7 = (f32[4,8,128]{2,1,0:T(8,128)S(1)}, f32[4,8,128]{2,1,0:T(8,128)}, u32[]{:S(2)}) copy-start(f32[4,8,128]{2,1,0:T(8,128)} %get-tuple-element.42.refs_16_) | copy-start | bytes 49156

commit v3 on v2

v3 whole, which is shorter than its diff:
```python
import functools
import math

import jax
import jax.numpy as jnp
from jax import lax
from jax.experimental import pallas as pl
from jax.experimental.pallas import tpu as pltpu
from jax.sharding import PartitionSpec as P

HD = 128
PAGE = 16
CAP = 2
CUT = 1024
NORM_EPSILON = 1e-05
ROPE_THETA = 500000.0
LOW = -1e30
EXP2_SCALE = math.log2(math.e) / math.sqrt(HD)
VMEM_BYTES = 32 * 1024 * 1024
NT = (((1,), (1,)), ((), ()))


def params(limit=VMEM_BYTES):
    return pltpu.CompilerParams(vmem_limit_bytes=limit)


def stage_kernel(n_arrays, *refs):
    copies = [
        pltpu.make_async_copy(refs[i], refs[n_arrays + i], refs[2 * n_arrays].at[i])
        for i in range(n_arrays)
    ]
    for copy in copies:
        copy.start()
    for copy in copies:
        copy.wait()


def stage(*arrays):
    return pl.pallas_call(
        functools.partial(stage_kernel, len(arrays)),
        out_shape=tuple(jax.ShapeDtypeStruct(a.shape, a.dtype) for a in arrays),
        in_specs=[pl.BlockSpec(memory_space=pl.ANY)] * len(arrays),
        out_specs=[pl.BlockSpec(memory_space=pltpu.VMEM)] * len(arrays),
        scratch_shapes=[pltpu.SemaphoreType.DMA((len(arrays),))],
        compiler_params=params(),
        cost_estimate=pl.CostEstimate(
            flops=0, bytes_accessed=sum(2 * a.size * a.dtype.itemsize for a in arrays), transcendentals=0
        ),
        name="stage",
    )(*arrays)


def project_kernel(n_parts, chunk, order_ref, *refs):
    parts = refs[:n_parts]
    gain_ref, key_ref, value_ref, cos_ref, sin_ref, column_ref, row_ref = refs[n_parts:-2]
    out_ref, total_ref = refs[-2:]
    rows, part_width = parts[0].shape
    key_width = key_ref.shape[1]
    pages = column_ref.shape[0]
    earlier = lax.broadcasted_iota(jnp.int32, (pages, pages), 1) < lax.broadcasted_iota(
        jnp.int32, (pages, pages), 0
    )
    same = earlier & (column_ref[...] == row_ref[...])
    rank = jnp.sum(same.astype(jnp.float32), axis=1, keepdims=True)
    codes = column_ref[...].astype(jnp.float32) * CAP + rank
    out_ref[rows:] = jnp.broadcast_to(codes, (pages, 2 * key_width)).astype(jnp.bfloat16)
    squares = jnp.zeros((rows, HD), jnp.float32)
    for part in parts:
        for first in range(0, part_width, HD):
            piece = part[:, first : first + HD].astype(jnp.float32)
            squares += piece * piece
    squares = jnp.sum(squares, axis=1, keepdims=True)
    inverse = lax.rsqrt(squares * (1.0 / (part_width * n_parts)) + NORM_EPSILON)
    for index, part in enumerate(parts):
        base = order_ref[index] * part_width
        for first in range(0, part_width, chunk):
            where = pl.multiple_of(base + first, chunk)
            piece = part[:, first : first + chunk].astype(jnp.float32)
            normed = (piece * inverse * gain_ref[:, pl.ds(where, chunk)]).astype(jnp.bfloat16)
            keys = jnp.dot(
                normed, key_ref[pl.ds(where, chunk)], preferred_element_type=jnp.float32
            )
            values = jnp.dot(
                normed, value_ref[pl.ds(where, chunk)], preferred_element_type=jnp.float32
            )
            if index == 0 and first == 0:
                total_ref[:, :key_width] = keys
                total_ref[:, key_width:] = values
            else:
                total_ref[:, :key_width] += keys
                total_ref[:, key_width:] += values
    for head in range(key_width // HD):
        cut = slice(head * HD, (head + 1) * HD)
        raw = total_ref[:, cut]
        turned = raw * cos_ref[...] + pltpu.roll(raw, HD // 2, 1) * sin_ref[...]
        out_ref[:rows, cut] = turned.astype(jnp.bfloat16)
    out_ref[:rows, key_width:] = total_ref[:, key_width:].astype(jnp.bfloat16)


def project(parts, order, norm_gain, key_weight, value_weight, cosine, sine, page_owner):
    rows, part_width = parts[0].shape
    n_parts = len(parts)
    key_width = key_weight.shape[1]
    vmem = pl.BlockSpec(memory_space=pltpu.VMEM)
    pages = page_owner.shape[0]
    return pl.pallas_call(
        functools.partial(project_kernel, n_parts, math.gcd(part_width, 1024)),
        out_shape=jax.ShapeDtypeStruct((rows + pages, 2 * key_width), jnp.bfloat16),
        in_specs=[pl.BlockSpec(memory_space=pltpu.SMEM)] + [vmem] * (n_parts + 7),
        out_specs=vmem,
        scratch_shapes=[pltpu.VMEM((rows, 2 * key_width), jnp.float32)],
        compiler_params=params(),
        cost_estimate=pl.CostEstimate(
            flops=4 * rows * key_width * part_width * n_parts,
            bytes_accessed=4 * key_width * part_width * n_parts,
            transcendentals=0,
        ),
        name="project",
    )(
        order,
        *parts,
        norm_gain.reshape(1, -1),
        key_weight,
        value_weight,
        cosine,
        sine,
        page_owner.reshape(-1, 1),
        page_owner.reshape(1, -1),
    )


def stack_heads(ref, group):
    return jnp.concatenate([ref[:, h * HD : (h + 1) * HD] for h in range(group)], axis=0)


def turned_with_ones(values):
    turned = values.T
    return jnp.concatenate([turned, jnp.ones((16, turned.shape[1]), turned.dtype)], axis=0)


def counted_piece(queries, keys, values_ones, bias, old_max):
    scores = lax.dot_general(keys, queries, NT, preferred_element_type=jnp.float32)
    scores = scores * EXP2_SCALE + bias
    new_max = jnp.maximum(old_max, jnp.max(scores, axis=0, keepdims=True))
    weights = jnp.exp2(scores - new_max).astype(jnp.bfloat16)
    product = jnp.dot(values_ones, weights, preferred_element_type=jnp.float32)
    return new_max, product


def store_stats(stat_ref, columns, row_max, row_sum):
    stat_ref[0, 0:1, columns] = row_max
    stat_ref[0, 1:2, columns] = row_sum


def page_bias(ids, table_ref, length, store):
    pages, lanes = ids.shape
    found = jnp.zeros((pages, lanes), jnp.int32)
    for entry in range(table_ref.shape[0]):
        left = length - entry * PAGE
        weight = jnp.where(left >= PAGE, 1, jnp.where(left > 0, CUT, 0))
        found += jnp.where(ids == table_ref[entry : entry + 1, :], weight, 0)

    def logarithm(count):
        return jnp.where(count > 0, jnp.log2(jnp.maximum(count, 1).astype(jnp.float32)), LOW)

    whole = found & (CUT - 1)
    with_cut = logarithm(whole + lax.shift_right_logical(found, CUT.bit_length() - 1))
    whole = logarithm(whole)
    token = lax.broadcasted_iota(jnp.int32, (PAGE, lanes), 0)
    kept = token < length % PAGE
    for page in range(pages):
        one = slice(page, page + 1)
        store(page, jnp.where(kept, with_cut[one], whole[one]))


def resident_kernel(
    group, pool, slot_ref, query_ref, key_ref, value_ref, table_ref, length_ref, *refs
):
    acc_ref, stat_ref, slot_bias_ref, bias = refs
    step = pl.program_id(0)
    pages, lanes = bias.shape[0] // PAGE, bias.shape[1]

    @pl.when(step == 0)
    def _():
        acc_ref[...] = jnp.zeros_like(acc_ref)
        stat_ref[:, 0:1] = jnp.full_like(stat_ref[:, 0:1], LOW)
        stat_ref[:, 1:2] = jnp.zeros_like(stat_ref[:, 1:2])
        slots = slot_bias_ref.shape[0] // PAGE
        slot_of = lax.broadcasted_iota(jnp.int32, (slots, lanes), 0)
        ids = slot_of % CAP
        for block in range(slots // CAP):
            ids += jnp.where(slot_of // CAP == block, pool + slot_ref[block] * CAP, 0)

        def store_slot(page, found):
            slot_bias_ref[page * PAGE : (page + 1) * PAGE] = found

        page_bias(ids, table_ref, length_ref[...], store_slot)

    def store(page, found):
        bias[page * PAGE : (page + 1) * PAGE] = found

    ids = step * pages + lax.broadcasted_iota(jnp.int32, (pages, lanes), 0)
    page_bias(ids, table_ref, length_ref[...], store)
    for head in range(key_ref.shape[1] // HD):
        cut = slice(head * HD, (head + 1) * HD)
        queries = jnp.concatenate(
            [
                query_ref[:, (head * group + h) * HD : (head * group + h + 1) * HD]
                for h in range(group)
            ],
            axis=0,
        )
        old_max = stat_ref[head, 0:1]
        new_max, product = counted_piece(
            queries, key_ref[:, cut], turned_with_ones(value_ref[:, cut]), bias[...], old_max
        )
        fade = jnp.exp2(old_max - new_max)
        acc_ref[head] = acc_ref[head] * fade + product[:HD]
        stat_ref[head, 1:2] = stat_ref[head, 1:2] * fade + product[HD : HD + 1]
        stat_ref[head, 0:1] = new_max


def resident_attention(decode_query, keys, values, table, lengths, slots, pool):
    pool_rows, key_width = keys.shape
    kv_heads = key_width // HD
    group = decode_query.shape[1] // key_width
    lanes = table.shape[1]
    steps = math.gcd(pool, 4)
    chunk = pool_rows // steps

    def whole(*shape):
        return pl.BlockSpec(shape, lambda step, _: (0,) * len(shape))

    piece = pl.BlockSpec((chunk, key_width), lambda step, _: (step, 0))
    shapes = [(kv_heads, HD, lanes), (kv_heads, 8, lanes), (slots.shape[0] * CAP * PAGE, lanes)]
    return pl.pallas_call(
        functools.partial(resident_kernel, group, pool),
        out_shape=tuple(jax.ShapeDtypeStruct(shape, jnp.float32) for shape in shapes),
        grid_spec=pltpu.PrefetchScalarGridSpec(
            num_scalar_prefetch=1,
            grid=(steps,),
            in_specs=[whole(*decode_query.shape), piece, piece]
            + [whole(*table.shape), whole(*lengths.shape)],
            out_specs=[whole(*shape) for shape in shapes],
            scratch_shapes=[pltpu.VMEM((chunk, lanes), jnp.float32)],
        ),
        compiler_params=params(60 * 2**20),
        cost_estimate=pl.CostEstimate(
            flops=6 * kv_heads * lanes * pool_rows * HD,
            bytes_accessed=4 * key_width * pool_rows,
            transcendentals=kv_heads * lanes * pool_rows,
        ),
        name="resident",
    )(slots, decode_query, keys, values, table, lengths)


def pages_here(code_ref, key_ref, value_ref, own, rows):
    codes = code_ref[...].astype(jnp.float32).astype(jnp.int32)
    found = []
    for slot in range(CAP):
        mine = codes == own * CAP + slot
        both = [jnp.zeros((PAGE, HD), jnp.float32)] * 2
        for page in range(rows // PAGE):
            here = jnp.broadcast_to(mine[page : page + 1], (PAGE, HD))
            cut = slice(page * PAGE, (page + 1) * PAGE)
            both = [
                jnp.where(here, ref[cut].astype(jnp.float32), held)
                for ref, held in zip((key_ref, value_ref), both)
            ]
        found.append(jnp.concatenate(both, axis=1))
    return jnp.concatenate(found, axis=0).astype(jnp.bfloat16)


def attend_kernel(n_blocks, n_pages, group, first, final, place_ref, *refs):
    refs = list(refs)

    def take(count):
        taken, refs[:count] = refs[:count], []
        return taken

    (query_ref,) = take(1)
    keys = take(n_blocks)
    values = take(n_blocks)
    codes = take(n_blocks)
    if not first:
        acc_in, stat_in = take(2)
    if final:
        decode_ref, side_acc, side_stat, bias_ref = take(4)
        pages = take(n_pages)
        out_ref, decode_out = refs
    else:
        acc_out, stat_out, page_out = refs
    rows = query_ref.shape[0]
    own = place_ref[0]
    all_keys = jnp.concatenate([ref[...] for ref in keys], axis=0)
    all_values = turned_with_ones(jnp.concatenate([ref[...] for ref in values], axis=0))
    seen = [place_ref[1 + b] < own for b in range(n_blocks)]
    span = rows
    queries = stack_heads(query_ref, group)
    scores = lax.dot_general(all_keys, queries, NT, preferred_element_type=jnp.float32)
    pieces = [scores[b * span : (b + 1) * span] for b in range(n_blocks)]
    if first:
        key_of = lax.broadcasted_iota(jnp.int32, (span, rows), 0)
        row_of = lax.broadcasted_iota(jnp.int32, (span, rows), 1)
        kept = jnp.concatenate([key_of <= row_of] * group, axis=1)
        pieces[0] = jnp.where(kept, pieces[0], LOW)
        new_max = jnp.max(pieces[0], axis=0, keepdims=True) * EXP2_SCALE
    else:
        old_max = stat_in[0, 0:1]
        new_max = old_max
    for b in range(1 if first else 0, n_blocks):
        highest = jnp.max(pieces[b], axis=0, keepdims=True) * EXP2_SCALE
        new_max = jnp.maximum(new_max, jnp.where(seen[b], highest, LOW))
    weights = []
    for b in range(n_blocks):
        shift = new_max
        if not (first and b == 0):
            shift = new_max + jnp.where(seen[b], 0.0, -LOW)
        weights.append(jnp.exp2(pieces[b] * EXP2_SCALE - shift).astype(jnp.bfloat16))
    product = jnp.dot(
        all_values, jnp.concatenate(weights, axis=0), preferred_element_type=jnp.float32
    )
    acc, total = product[:HD], product[HD : HD + 1]
    if not first:
        fade = jnp.exp2(old_max - new_max)
        acc += acc_in[0] * fade
        total += stat_in[0, 1:2] * fade
    new_pages = jnp.concatenate(
        [pages_here(codes[b], keys[b], values[b], own, rows) for b in range(n_blocks)], axis=0
    )
    if not final:
        acc_out[0] = acc
        store_stats(stat_out, slice(None), new_max, total)
        page_out[0] = new_pages
        return

    result = (acc * (1.0 / total)).astype(jnp.bfloat16)
    for h in range(group):
        out_ref[:, h * HD : (h + 1) * HD] = (
            result[:, h * rows : (h + 1) * rows].T
        )

    decode_rows = decode_ref.shape[0]

    all_pages = jnp.concatenate([ref[0] for ref in pages] + [new_pages], axis=0)
    queries = stack_heads(decode_ref, group)
    side_max = side_stat[0, 0:1]
    new_max, product = counted_piece(
        queries,
        all_pages[:, :HD],
        turned_with_ones(all_pages[:, HD:]),
        bias_ref[...],
        side_max,
    )
    fade = jnp.exp2(side_max - new_max)
    acc = product[:HD] + side_acc[0] * fade
    total = product[HD : HD + 1] + side_stat[0, 1:2] * fade
    result = (acc / total).T.astype(jnp.bfloat16)
    for h in range(group):
        decode_out[:, h * HD : (h + 1) * HD] = result[h * decode_rows : (h + 1) * decode_rows]


def attend(arrived, section, query, state, decode, kv_heads):
    blocks = [block for block, _ in arrived]
    place = jnp.stack([section] + [s.astype(jnp.int32) for _, s in arrived])
    n_blocks = len(blocks)
    rows, query_width = query.shape
    group = query_width // (kv_heads * HD)
    pages = blocks[0].shape[0] - rows
    first, final = state is None, decode is not None
    total_rows = group * rows
    page_rows = n_blocks * CAP * PAGE

    def by_head(*shape):
        return pl.BlockSpec((1, *shape), lambda g, *_: (g, 0, 0))

    def whole(array):
        return pl.BlockSpec(array.shape, lambda g, *_: (0, 0))

    query_spec = pl.BlockSpec((rows, group * HD), lambda g, *_: (0, g))
    key_spec = pl.BlockSpec((rows, HD), lambda g, *_: (0, g))
    value_spec = pl.BlockSpec((rows, HD), lambda g, *_: (0, kv_heads + g))
    code_spec = pl.BlockSpec((pages, HD), lambda g, *_: (rows // pages, 0))
    operands = [query, *blocks, *blocks, *blocks]
    in_specs = [query_spec] + [key_spec] * n_blocks + [value_spec] * n_blocks
    in_specs += [code_spec] * n_blocks
    held = []
    if not first:
        acc, stats, held = state
        operands += [acc, stats]
        in_specs += [by_head(HD, total_rows), by_head(8, total_rows)]
    if final:
        decode_query, side_acc, side_stat, bias = decode
        small = bias.shape[1]
        decode_spec = pl.BlockSpec((decode_query.shape[0], group * HD), lambda g, *_: (0, g))
        operands += [decode_query, side_acc, side_stat, bias, *held]
        in_specs += [decode_spec, by_head(HD, small), by_head(8, small), whole(bias)]
        in_specs += [by_head(*array.shape[1:]) for array in held]
        out_shape = (
            jax.ShapeDtypeStruct(query.shape, jnp.bfloat16),
            jax.ShapeDtypeStruct(decode_query.shape, jnp.bfloat16),
        )
        out_specs = [query_spec, decode_spec]
    else:
        out_shape = (
            jax.ShapeDtypeStruct((kv_heads, HD, total_rows), jnp.float32),
            jax.ShapeDtypeStruct((kv_heads, 8, total_rows), jnp.float32),
            jax.ShapeDtypeStruct((kv_heads, page_rows, 2 * HD), jnp.bfloat16),
        )
        out_specs = [by_head(*shape.shape[1:]) for shape in out_shape]
    pairs = kv_heads * total_rows * n_blocks * rows
    result = pl.pallas_call(
        functools.partial(attend_kernel, n_blocks, len(held), group, first, final),
        out_shape=out_shape,
        grid_spec=pltpu.PrefetchScalarGridSpec(
            num_scalar_prefetch=1,
            grid=(kv_heads,),
            in_specs=in_specs,
            out_specs=out_specs,
        ),
        compiler_params=params(),
        cost_estimate=pl.CostEstimate(
            flops=6 * pairs * HD,
            bytes_accessed=12 * kv_heads * total_rows * HD,
            transcendentals=pairs,
        ),
        name="attend",
    )(place, *operands)
    if final:
        return result
    return result[0], result[1], [*held, result[2]]


def fence(*arrays):
    return lax.optimization_barrier(arrays)


def grid_sections():
    here = lax.axis_index("section")
    z, column = here // 4, here % 4
    inner = (z == 1) | (z == 2)
    plane_a = jnp.bitwise_xor(z, 1)
    plane_f = jnp.where(inner, 3 - z, jnp.where(z == 0, 2, 1))
    plane_g = jnp.where(inner, jnp.bitwise_xor(3 - z, 1), 3 - z)
    order = [(z, 0), (z, 1), (z, 2), (plane_a, 0), (z, 3), (plane_a, 2), (plane_f, 0)]
    order += [(plane_a, 1), (plane_f, 2), (plane_g, 0), (plane_f, 1), (plane_g, 2), (plane_f, 3)]
    order += [(plane_g, 1), (plane_a, 3), (plane_g, 3)]
    return [plane * 4 + jnp.bitwise_xor(column, turn) for plane, turn in order]


def gather_rounds(own, sections, work):
    sections = iter(sections)

    def named(*blocks):
        return [(block, next(sections)) for block in blocks]

    def settle(moved, work, *kept):
        return fence(*moved, *kept, *work)[: len(moved) + len(kept)]

    size_z, size_y, size_x = 4, 2, 2
    z = lax.axis_index("section") // 4

    def index(zz, yy, xx):
        return (zz * size_y + yy) * size_x + xx

    def along_z(pairs):
        return [
            (index(a, yy, xx), index(b, yy, xx))
            for a, b in pairs
            for yy in range(size_y)
            for xx in range(size_x)
        ]

    every = [(zz, yy, xx) for zz in range(size_z) for yy in range(size_y) for xx in range(size_x)]
    swap_x = [(index(zz, yy, xx), index(zz, yy, 1 - xx)) for zz, yy, xx in every]
    swap_y = [(index(zz, yy, xx), index(zz, 1 - yy, xx)) for zz, yy, xx in every]
    ends = along_z([(0, 1), (1, 0), (2, 3), (3, 2)])
    middle = along_z([(1, 2), (2, 1)])
    outward = along_z([(1, 0), (2, 3)])
    inner = (z == 1) | (z == 2)

    def move(block, pairs):
        return lax.ppermute(block, "section", pairs)

    moved = move(own, swap_x), move(own, swap_y), move(own, ends), move(own, middle)
    own_x, own_y, a, b = settle(moved, work)
    work = yield named(own, own_x, own_y, a)
    moved = move(own_y, swap_x), move(a, swap_y), move(b, outward), move(a, middle)
    own_d, a_y, c, d, a, b = settle(moved, work, a, b)
    f = jnp.where(inner, b, c)
    work = yield named(own_d, a_y, f)
    either = jnp.where(inner, d, own_d)
    moved = move(a, swap_x), move(f, swap_y), move(either, ends), move(own_d, middle)
    a_x, f_y, e, b_in, f, d = settle(moved, work, f, d)
    g = jnp.where(inner, d, e)
    work = yield named(a_x, f_y, g)
    moved = move(f, swap_x), move(g, swap_y), move(b_in, outward), move(e, middle)
    f_x, g_y, c_in, d_in, g, a_x, b_in, e = settle(moved, work, g, a_x, b_in, e)
    f_d = jnp.where(inner, b_in, c_in)
    work = yield named(f_x, g_y, f_d)
    moved = move(g, swap_x), move(a_x, swap_y), move(d_in, outward)
    g_x, a_turn, e_in = settle(moved, work)
    a_d = jnp.where(inner, e, a_turn)
    g_d = jnp.where(inner, d_in, e_in)
    yield named(g_x, a_d, g_d)


def plain_sections(section_count, section, pool):
    every = [jnp.int32(s) for s in range(section_count)]
    return [jnp.where(s == section, -pool, s) for s in every]


def gather_plain(own, section_count):
    rows = own.shape[0]
    gathered = lax.all_gather(own, "section", axis=0, tiled=True)
    step = math.gcd(section_count, 4)
    for top in range(0, section_count, step):
        yield [
            (gathered[s * rows : (s + 1) * rows], jnp.int32(s)) for s in range(top, top + step)
        ]


def per_device(
    prefill_hidden,
    norm_gain,
    key_weight,
    value_weight,
    prefill_query,
    resident_keys,
    resident_values,
    decode_query,
    page_owner,
    block_table,
    context_len,
):
    section_count = lax.axis_size("section")
    tp_count = lax.axis_size("tp")
    section = lax.axis_index("section").astype(jnp.int32)
    tp = lax.axis_index("tp").astype(jnp.int32)
    rows = prefill_hidden.shape[0]
    key_width = key_weight.shape[1]
    kv_heads = key_width // HD
    group = prefill_query.shape[1] // key_width
    pool = resident_keys.shape[0]

    if tp_count == 2:
        other = lax.ppermute(prefill_hidden, "tp", [(0, 1), (1, 0)])
        parts, order = [prefill_hidden, other], jnp.stack([tp, 1 - tp])
    else:
        parts = [lax.all_gather(prefill_hidden, "tp", axis=1, tiled=True)]
        order = jnp.zeros((1,), jnp.int32)
    half = HD // 2
    frequency = jnp.exp(jnp.arange(half, dtype=jnp.float32) * (-2.0 * math.log(ROPE_THETA) / HD))
    positions = section * rows + jnp.arange(rows, dtype=jnp.int32)
    angles = positions.astype(jnp.float32)[:, None] * frequency[None, :]
    cosine, sine = jnp.cos(angles), jnp.sin(angles)
    cosine = jnp.concatenate([cosine, cosine], axis=1)
    sine = jnp.concatenate([-sine, sine], axis=1)

    key_near, value_near = stage(key_weight, value_weight)
    own = project(
        parts, order, norm_gain, key_near, value_near, cosine, sine, page_owner
    )

    own, block_table, context_len = fence(own, block_table, context_len)
    table = jnp.concatenate([block_table] * group, axis=0).T
    lengths = jnp.concatenate([context_len] * group)[None, :]
    if section_count == 16:
        sections = grid_sections()
    else:
        sections = [section] + plain_sections(section_count, section, pool)
    decode = (
        decode_query,
        *resident_attention(
            decode_query,
            resident_keys.reshape(pool * PAGE, key_width),
            resident_values.reshape(pool * PAGE, key_width),
            table,
            lengths,
            jnp.stack(sections).astype(jnp.int32),
            pool,
        ),
    )

    def step(arrived, state, last=False):
        return attend(arrived, section, prefill_query, state, decode if last else None, kv_heads)

    if section_count == 16:
        rounds = gather_rounds(own, sections, decode[1:])
        arrived, state = next(rounds), None
        for _ in range(4):
            state = step(arrived, state)
            arrived = rounds.send((state[0], state[1]))
        return step(arrived, state, True)
    state = step([(own, section)], None)
    rounds = list(gather_plain(own, section_count))
    for arrived in rounds[:-1]:
        state = step(arrived, state)
    return step(rounds[-1], state, True)


def solution(mesh):
    return jax.shard_map(
        per_device,
        mesh=mesh,
        in_specs=(
            P("section", "tp"),
            P(),
            P(None, "tp"),
            P(None, "tp"),
            P("section", "tp"),
            P("section", None, "tp"),
            P("section", None, "tp"),
            P("section", "tp"),
            P("section"),
            P("section", None),
            P("section"),
        ),
        out_specs=(P("section", "tp"), P("section", "tp")),
        check_vma=False,
    )
```

time: 139 us -> 122 us (0.88)
  Pallas kernels: 95.7 us -> 83.5 us
  waiting for transfers between devices: 5.87 us -> 1.66 us
  other arithmetic: 2.95 us -> 1.38 us
  local copies, waits for them, and re-layouts: 3.25 us -> 4.65 us
    pallas_call x6, Pallas kernels: 83.9 us -> 71.6 us  [the longest x5 62.8 us: attend(): pl.pallas_call(functools.partial(attend_kernel, n_blocks, len(held), grou...]
    ppermute x19, waiting for transfers between devices: 5.86 us -> 1.66 us  [move(): return lax.ppermute(block, 'section', pairs)]
  transfers between devices with their start and end apart: 20 -> 20, of which waited for: 1 -> 3; matrix products, arithmetic and copies ran while one was open for 3% -> 4% of each run, Pallas kernels for 53% -> 52%
where the time goes in v3:
time: 122 us; the launch traced here: 121 us
  Pallas kernels  83.5 us (68%)
  starting transfers between devices  29.2 us (24%)
  local copies, waits for them, and re-layouts  4.65 us (4%)
  waiting for transfers between devices  1.66 us (1%)
  other arithmetic  1.38 us (1%)
    pallas_call x5, Pallas kernels, attend(): pl.pallas_call(functools.partial(attend_kernel, n_blocks, len(held), grou...  62.8 us
    ppermute x19, starting transfers between devices, move(): return lax.ppermute(block, 'section', pairs)  28.7 us
    pallas_call x1, Pallas kernels, resident_attention(): pl.pallas_call(functools.partial(resident_kernel, group, pool), out_shape...  8.75 us
    pallas_call x1, Pallas kernels, project(): pl.pallas_call(functools.partial(project_kernel, n_parts, math.gcd(part_w...  5.95 us
    pallas_call x1, Pallas kernels, stage(): pl.pallas_call(functools.partial(stage_kernel, len(arrays)), out_shape=tu...  5.93 us
  transfers between devices with their start and end apart: 20, of which 3 were waited for; matrix products, arithmetic and copies ran while one was open for 4% of the time, Pallas kernels for 52%

profile of v3, /device:TPU:0, one launch (start us, length us, event | category | flops | bytes accessed | tf_op | source)
XLA Modules:
  0.0 121.4 jit_solution(9450286399807141120)
XLA Ops:
  0.6 0.5 collective-permute-start
  1.1 0.7 copy.13.refs_7_
  1.9 5.9 %stage.1 = (bf16[8192,512]{1,0:T(8,128)(2,1)S(1)}, bf16[8192,512]{1,0:T(8,128)(2,1)S(1)}) custom-call(bf16[8192,512]{1,0:T(8,128)(2,1)} %refs_0_.7, bf16[8192,512]{1,0:T(8,128)(2,1)} %refs_1_.1), custom_call_target="tpu_custom_call" | custom-call | bytes 33554432 | tf_op jit(solution)/shard_map/stage/pallas_call | solution.py:39
  7.8 0.1 pad_add_fusion.1.order_ref
  7.9 0.5 fusion
  8.5 0.1 pad_maximum_fusion
  8.7 5.9 %project.1.refs_1_.refs_5_.refs_9_ = bf16[272,1024]{1,0:T(8,128)(2,1)S(1)} custom-call(s32[2]{0:T(128)S(1)} %pad_add_fusion.1.order_ref, bf16[256,4096]{1,0:T(8,128)(2,1)S(1)} %copy-done, bf16[256,4096]{1,0:T(8,128)(2,1)S(1)} %collective-permute-done.refs_1_, f32[1,8192]{1,0:T(1,128)S(1)} %bitcast.26, bf16[8192,512]{1,0:T(8,128)(2,1)S(1)} %get-tuple-element.49.refs_3_, ...), custom_call_target="tpu_custom_call" | custom-call | flops 4294967296 | bytes 16777216 | tf_op jit(solution)/shard_map/project/pallas_call | solution.py:106
  14.6 0.7 collective-permute-start.4
  15.3 5.5 %collective-permute-start.3 = (bf16[272,1024]{1,0:T(8,128)(2,1)S(1)}, bf16[272,1024]{1,0:T(8,128)(2,1)S(1)}, u32[]{:S(2)}, u32[]{:S(2)}) collective-permute-start(bf16[272,1024]{1,0:T(8,128)(2,1)S(1)} %project.1.refs_1_.refs_5_.refs_9_), channel_id=1, source_target_pairs={{0,8},{2,10},{4,12},{6,14},{8,0},{10,2},{12,4},{14,6},{16,24},{18,... | collective-permute-start | bytes 1671176 | tf_op jit(solution)/shard_map/ppermute | solution.py:483
  20.8 1.5 %collective-permute-start.2 = (bf16[272,1024]{1,0:T(8,128)(2,1)S(1)}, bf16[272,1024]{1,0:T(8,128)(2,1)S(1)}, u32[]{:S(2)}, u32[]{:S(2)}) collective-permute-start(bf16[272,1024]{1,0:T(8,128)(2,1)S(1)} %project.1.refs_1_.refs_5_.refs_9_), channel_id=1, source_target_pairs={{0,4},{2,6},{4,0},{6,2},{8,12},{10,14},{12,8},{14,10},{16,20},{18,... | collective-permute-start | bytes 1671176 | tf_op jit(solution)/shard_map/ppermute | solution.py:483
  22.3 1.5 %collective-permute-start.1 = (bf16[272,1024]{1,0:T(8,128)(2,1)S(1)}, bf16[272,1024]{1,0:T(8,128)(2,1)S(1)}, u32[]{:S(2)}, u32[]{:S(2)}) collective-permute-start(bf16[272,1024]{1,0:T(8,128)(2,1)S(1)} %project.1.refs_1_.refs_5_.refs_9_), channel_id=1, source_target_pairs={{0,2},{2,0},{4,6},{6,4},{8,10},{10,8},{12,14},{14,12},{16,18},{18,... | collective-permute-start | bytes 1671176 | tf_op jit(solution)/shard_map/ppermute | solution.py:483
  23.8 0.1 stack.120.place_ref
  23.9 0.7 stack.119.slot_ref
  24.6 0.1 pad_add_fusion.2
  24.6 0.7 concatenate.15
  25.3 0.1 copy.14
  25.4 0.7 concatenate.14
  26.2 8.8 %resident.1 = (f32[4,128,128]{2,1,0:T(8,128)}, f32[4,8,128]{2,1,0:T(8,128)}, f32[512,128]{1,0:T(8,128)}) custom-call(s32[16]{0:T(128)} %stack.119.slot_ref, bf16[16,4096]{1,0:T(8,128)(2,1)} %refs_12_.1, bf16[4096,512]{1,0:T(8,128)(2,1)} %bitcast.29, bf16[4096,512]{1,0:T(8,128)(2,1)} %bitcast.30, s32[62,128]{1,0:T(8,128)} %bitcast.31, s32[1,128]{1,0:T(1,128)} %bitcast.32), custom_call_target="tpu_custom_call" | custom-call | flops 1610612736 | bytes 8388608 | tf_op jit(solution)/shard_map/resident/pallas_call | solution.py:236
  34.9 0.3 collective-permute-done.2.refs_3_.refs_7_.refs_11_
  35.2 1.2 %collective-permute-done.1.refs_2_.refs_6_.refs_10_ = bf16[272,1024]{1,0:T(8,128)(2,1)S(1)} collective-permute-done((bf16[272,1024]{1,0:T(8,128)(2,1)S(1)}, bf16[272,1024]{1,0:T(8,128)(2,1)S(1)}, u32[]{:S(2)}, u32[]{:S(2)}) %collective-permute-start.1) | collective-permute-done | bytes 557088 | tf_op jit(solution)/shard_map/ppermute | solution.py:483
  36.5 0.7 collective-permute-start.8
  37.2 0.6 collective-permute-start.6
  37.7 1.5 %collective-permute-start.5 = (bf16[272,1024]{1,0:T(8,128)(2,1)S(1)}, bf16[272,1024]{1,0:T(8,128)(2,1)S(1)}, u32[]{:S(2)}, u32[]{:S(2)}) collective-permute-start(bf16[272,1024]{1,0:T(8,128)(2,1)S(1)} %collective-permute-done.2.refs_3_.refs_7_.refs_11_), channel_id=1, source_target_pairs={{0,2},{2,0},{4,6},{6,4},{8,10},{10,8},{12,14},{14,12},{16,18},{18,... | collective-permute-start | bytes 1671176 | tf_op jit(solution)/shard_map/ppermute | solution.py:483
  39.2 1.3 %collective-permute-start.7 = (bf16[272,1024]{1,0:T(8,128)(2,1)S(1)}, bf16[272,1024]{1,0:T(8,128)(2,1)S(1)}, u32[]{:S(2)}, u32[]{:S(2)}) collective-permute-start(bf16[272,1024]{1,0:T(8,128)(2,1)S(1)} %collective-permute-done.4), channel_id=1, source_target_pairs={{8,0},{10,2},{12,4},{14,6},{16,24},{18,26},{20,28},{22,30},{9,1},{... | collective-permute-start | bytes 1671176 | tf_op jit(solution)/shard_map/ppermute | solution.py:483
  40.5 1.6 %copy-done.4 = bf16[256,4096]{1,0:T(8,128)(2,1)S(1)} copy-done((bf16[256,4096]{1,0:T(8,128)(2,1)S(1)}, bf16[256,4096]{1,0:T(8,128)(2,1)}, u32[]{:S(2)}) %copy-start.4) | copy-done | bytes 2097176
  42.1 13.2 %attend.5 = (f32[4,128,2048]{2,1,0:T(8,128)S(1)}, f32[4,8,2048]{2,1,0:T(8,128)S(1)}, bf16[4,128,256]{2,1,0:T(8,128)(2,1)S(1)}) custom-call(s32[5]{0:T(128)S(1)} %stack.120.place_ref, bf16[256,4096]{1,0:T(8,128)(2,1)S(1)} %copy-done.4, bf16[272,1024]{1,0:T(8,128)(2,1)S(1)} %project.1.refs_1_.refs_5_.refs_9_, ...), custom_call_target="tpu_custom_call" | custom-call | flops 6442450944 | bytes 12582912 | tf_op jit(solution)/shard_map/attend/pallas_call | solution.py:412
  55.3 0.9 collective-permute-start.12
  56.3 4.9 %collective-permute-start.11 = (bf16[272,1024]{1,0:T(8,128)(2,1)S(1)}, bf16[272,1024]{1,0:T(8,128)(2,1)S(1)}, u32[]{:S(2)}, u32[]{:S(2)}) collective-permute-start(bf16[272,1024]{1,0:T(8,128)(2,1)S(1)} %broadcast_select_fusion.4), channel_id=1, source_target_pairs={{0,8},{2,10},{4,12},{6,14},{8,0},{10,2},{12,4},{14,6},{16,24},{18,... | collective-permute-start | bytes 1671176 | tf_op jit(solution)/shard_map/ppermute | solution.py:483
  61.2 0.1 broadcast_select_fusion.5.refs_3_.refs_6_.refs_9_
  61.3 1.6 %collective-permute-start.10 = (bf16[272,1024]{1,0:T(8,128)(2,1)S(1)}, bf16[272,1024]{1,0:T(8,128)(2,1)S(1)}, u32[]{:S(2)}, u32[]{:S(2)}) collective-permute-start(bf16[272,1024]{1,0:T(8,128)(2,1)S(1)} %broadcast_select_fusion.5.refs_3_.refs_6_.refs_9_), channel_id=1, source_target_pairs={{0,4},{2,6},{4,0},{6,2},{8,12},{10,14},{12,8},{14,10},{16,20},{18,... | collective-permute-start | bytes 1671176 | tf_op jit(solution)/shard_map/ppermute | solution.py:483
  62.9 0.5 collective-permute-start.9
  63.4 0.1 pad_add_fusion.4.place_ref
  63.5 11.5 %attend.6 = (f32[4,128,2048]{2,1,0:T(8,128)S(1)}, f32[4,8,2048]{2,1,0:T(8,128)S(1)}, bf16[4,96,256]{2,1,0:T(8,128)(2,1)S(1)}) custom-call(s32[4]{0:T(128)S(1)} %get-tuple-element.99.place_ref, bf16[256,4096]{1,0:T(8,128)(2,1)S(1)} %copy-done.4, bf16[272,1024]{1,0:T(8,128)(2,1)S(1)} %collective-permute-done.5.refs_1_.refs_4_.refs_7_, ...), custom_call_target="tpu_custom_call" | custom-call | flops 4831838208 | bytes 12582912 | tf_op jit(solution)/shard_map/attend/pallas_call | solution.py:412
  75.1 0.7 collective-permute-start.16
  75.8 0.6 collective-permute-start.14
  76.4 1.5 %collective-permute-start.13 = (bf16[272,1024]{1,0:T(8,128)(2,1)S(1)}, bf16[272,1024]{1,0:T(8,128)(2,1)S(1)}, u32[]{:S(2)}, u32[]{:S(2)}) collective-permute-start(bf16[272,1024]{1,0:T(8,128)(2,1)S(1)} %broadcast_select_fusion.5.refs_3_.refs_6_.refs_9_), channel_id=1, source_target_pairs={{0,2},{2,0},{4,6},{6,4},{8,10},{10,8},{12,14},{14,12},{16,18},{18,... | collective-permute-start | bytes 1671176 | tf_op jit(solution)/shard_map/ppermute | solution.py:483
  77.9 1.3 %collective-permute-start.15 = (bf16[272,1024]{1,0:T(8,128)(2,1)S(1)}, bf16[272,1024]{1,0:T(8,128)(2,1)S(1)}, u32[]{:S(2)}, u32[]{:S(2)}) collective-permute-start(bf16[272,1024]{1,0:T(8,128)(2,1)S(1)} %collective-permute-done.12), channel_id=1, source_target_pairs={{8,0},{10,2},{12,4},{14,6},{16,24},{18,26},{20,28},{22,30},{9,1},{... | collective-permute-start | bytes 1671176 | tf_op jit(solution)/shard_map/ppermute | solution.py:483
  79.2 0.1 pad_add_fusion.place_ref
  79.3 11.6 %attend.7 = (f32[4,128,2048]{2,1,0:T(8,128)S(1)}, f32[4,8,2048]{2,1,0:T(8,128)S(1)}, bf16[4,96,256]{2,1,0:T(8,128)(2,1)S(1)}) custom-call(s32[4]{0:T(128)S(1)} %get-tuple-element.100.place_ref, bf16[256,4096]{1,0:T(8,128)(2,1)S(1)} %copy-done.4, bf16[272,1024]{1,0:T(8,128)(2,1)S(1)} %collective-permute-done.9.refs_1_.refs_4_.refs_7_, ...), custom_call_target="tpu_custom_call" | custom-call | flops 4831838208 | bytes 12582912 | tf_op jit(solution)/shard_map/attend/pallas_call | solution.py:412
  90.9 0.1 collective-permute-done.15
  91.0 0.5 collective-permute-start.17
  91.5 1.5 %collective-permute-start.18 = (bf16[272,1024]{1,0:T(8,128)(2,1)S(1)}, bf16[272,1024]{1,0:T(8,128)(2,1)S(1)}, u32[]{:S(2)}, u32[]{:S(2)}) collective-permute-start(bf16[272,1024]{1,0:T(8,128)(2,1)S(1)} %collective-permute-done.9.refs_1_.refs_4_.refs_7_), channel_id=1, source_target_pairs={{0,4},{2,6},{4,0},{6,2},{8,12},{10,14},{12,8},{14,10},{16,20},{18,... | collective-permute-start | bytes 1671176 | tf_op jit(solution)/shard_map/ppermute | solution.py:483
  93.0 1.5 %collective-permute-start.19 = (bf16[272,1024]{1,0:T(8,128)(2,1)S(1)}, bf16[272,1024]{1,0:T(8,128)(2,1)S(1)}, u32[]{:S(2)}, u32[]{:S(2)}) collective-permute-start(bf16[272,1024]{1,0:T(8,128)(2,1)S(1)} %collective-permute-done.16), channel_id=1, source_target_pairs={{8,0},{10,2},{12,4},{14,6},{16,24},{18,26},{20,28},{22,30},{9,1},{... | collective-permute-start | bytes 1671176 | tf_op jit(solution)/shard_map/ppermute | solution.py:483
  94.5 0.1 broadcast_select_fusion.2.refs_3_.refs_6_.refs_9_
  94.7 11.6 %attend.8 = (f32[4,128,2048]{2,1,0:T(8,128)S(1)}, f32[4,8,2048]{2,1,0:T(8,128)S(1)}, bf16[4,96,256]{2,1,0:T(8,128)(2,1)S(1)}) custom-call(s32[4]{0:T(128)S(1)} %pad_add_fusion.4.place_ref, bf16[256,4096]{1,0:T(8,128)(2,1)S(1)} %copy-done.4, bf16[272,1024]{1,0:T(8,128)(2,1)S(1)} %collective-permute-done.13.refs_1_.refs_4_.refs_7_, ...), custom_call_target="tpu_custom_call" | custom-call | flops 4831838208 | bytes 12582912 | tf_op jit(solution)/shard_map/attend/pallas_call | solution.py:412
  106.2 0.1 broadcast_select_fusion.refs_3_.refs_6_.refs_9_
  106.3 0.1 broadcast_select_fusion.1.refs_2_.refs_5_.refs_8_
  106.4 15.0 %attend.9 = (bf16[256,4096]{1,0:T(8,128)(2,1)}, bf16[16,4096]{1,0:T(8,128)(2,1)}) custom-call(s32[4]{0:T(128)S(1)} %pad_add_fusion.place_ref, bf16[256,4096]{1,0:T(8,128)(2,1)S(1)} %copy-done.4, bf16[272,1024]{1,0:T(8,128)(2,1)S(1)} %collective-permute-done.17.refs_1_.refs_4_.refs_7_, bf16[272,1024]{1,0:T(8,128)(2,1)S(1)} %broadcast_select_fusion.1.refs_2_.refs_5_.refs_8_, ...), custom_call_target="tpu_custom_call" | custom-call | flops 4831838208 | bytes 12582912 | tf_op jit(solution)/shard_map/attend/pallas_call | solution.py:412
  (40 shorter events, 0.2 us)
Async XLA Ops:
  0.6 8.0 %collective-permute-start = (bf16[256,4096]{1,0:T(8,128)(2,1)}, bf16[256,4096]{1,0:T(8,128)(2,1)S(1)}, u32[]{:S(2)}, u32[]{:S(2)}) collective-permute-start(bf16[256,4096]{1,0:T(8,128)(2,1)} %refs_0_.8), channel_id=1, source_target_pairs={{0,1},{1,0},{2,3},{3,2},{4,5},{5,4},{6,7},{7,6},{8,9},{9,8},{10,11... | collective-permute-start | bytes 6291464 | tf_op jit(solution)/shard_map/ppermute | solution.py:547
  1.9 6.7 %copy-start = (bf16[256,4096]{1,0:T(8,128)(2,1)S(1)}, bf16[256,4096]{1,0:T(8,128)(2,1)}, u32[]{:S(2)}) copy-start(bf16[256,4096]{1,0:T(8,128)(2,1)} %refs_0_.8) | copy-start | bytes 6291460
  1.9 6.8 %copy-start.2 = (f32[8192]{0:T(1024)S(1)}, f32[8192]{0:T(1024)}, u32[]{:S(2)}) copy-start(f32[8192]{0:T(1024)} %param.12) | copy-start | bytes 98308
  1.9 6.8 %copy-start.3 = (s32[16]{0:T(128)S(1)}, s32[16]{0:T(128)}, u32[]{:S(2)}) copy-start(s32[16]{0:T(128)} %param.19) | copy-start | bytes 196
  8.6 16.0 %copy-start.8 = (s32[16]{0:T(128)S(1)}, s32[16]{0:T(128)}, u32[]{:S(2)}) copy-start(s32[16]{0:T(128)} %param.21) | copy-start | bytes 196
  8.7 16.7 %copy-start.9 = (s32[16,62]{1,0:T(8,128)S(1)}, s32[16,62]{1,0:T(8,128)}, u32[]{:S(2)}) copy-start(s32[16,62]{1,0:T(8,128)} %param.20) | copy-start | bytes 11908
  14.6 20.3 %collective-permute-start.4 = (bf16[272,1024]{1,0:T(8,128)(2,1)S(1)}, bf16[272,1024]{1,0:T(8,128)(2,1)S(1)}, u32[]{:S(2)}, u32[]{:S(2)}) collective-permute-start(bf16[272,1024]{1,0:T(8,128)(2,1)S(1)} %project.1.refs_1_.refs_5_.refs_9_), channel_id=1, source_target_pairs={{8,16},{10,18},{12,20},{14,22},{16,8},{18,10},{20,12},{22,14},{9,1... | collective-permute-start | bytes 1671176 | tf_op jit(solution)/shard_map/ppermute | solution.py:483
  15.3 19.6 %collective-permute-start.3 = (bf16[272,1024]{1,0:T(8,128)(2,1)S(1)}, bf16[272,1024]{1,0:T(8,128)(2,1)S(1)}, u32[]{:S(2)}, u32[]{:S(2)}) collective-permute-start(bf16[272,1024]{1,0:T(8,128)(2,1)S(1)} %project.1.refs_1_.refs_5_.refs_9_), channel_id=1, source_target_pairs={{0,8},{2,10},{4,12},{6,14},{8,0},{10,2},{12,4},{14,6},{16,24},{18,... | collective-permute-start | bytes 1671176 | tf_op jit(solution)/shard_map/ppermute | solution.py:483
  20.8 14.4 %collective-permute-start.2 = (bf16[272,1024]{1,0:T(8,128)(2,1)S(1)}, bf16[272,1024]{1,0:T(8,128)(2,1)S(1)}, u32[]{:S(2)}, u32[]{:S(2)}) collective-permute-start(bf16[272,1024]{1,0:T(8,128)(2,1)S(1)} %project.1.refs_1_.refs_5_.refs_9_), channel_id=1, source_target_pairs={{0,4},{2,6},{4,0},{6,2},{8,12},{10,14},{12,8},{14,10},{16,20},{18,... | collective-permute-start | bytes 1671176 | tf_op jit(solution)/shard_map/ppermute | solution.py:483
  22.3 14.2 %collective-permute-start.1 = (bf16[272,1024]{1,0:T(8,128)(2,1)S(1)}, bf16[272,1024]{1,0:T(8,128)(2,1)S(1)}, u32[]{:S(2)}, u32[]{:S(2)}) collective-permute-start(bf16[272,1024]{1,0:T(8,128)(2,1)S(1)} %project.1.refs_1_.refs_5_.refs_9_), channel_id=1, source_target_pairs={{0,2},{2,0},{4,6},{6,4},{8,10},{10,8},{12,14},{14,12},{16,18},{18,... | collective-permute-start | bytes 1671176 | tf_op jit(solution)/shard_map/ppermute | solution.py:483
  36.5 18.8 %collective-permute-start.8 = (bf16[272,1024]{1,0:T(8,128)(2,1)S(1)}, bf16[272,1024]{1,0:T(8,128)(2,1)S(1)}, u32[]{:S(2)}, u32[]{:S(2)}) collective-permute-start(bf16[272,1024]{1,0:T(8,128)(2,1)S(1)} %collective-permute-done.3.refs_4_.refs_8_.refs_12_), channel_id=1, source_target_pairs={{8,16},{10,18},{12,20},{14,22},{16,8},{18,10},{20,12},{22,14},{9,1... | collective-permute-start | bytes 1671176 | tf_op jit(solution)/shard_map/ppermute | solution.py:483
  37.2 18.1 %collective-permute-start.6 = (bf16[272,1024]{1,0:T(8,128)(2,1)S(1)}, bf16[272,1024]{1,0:T(8,128)(2,1)S(1)}, u32[]{:S(2)}, u32[]{:S(2)}) collective-permute-start(bf16[272,1024]{1,0:T(8,128)(2,1)S(1)} %collective-permute-done.3.refs_4_.refs_8_.refs_12_), channel_id=1, source_target_pairs={{0,4},{2,6},{4,0},{6,2},{8,12},{10,14},{12,8},{14,10},{16,20},{18,... | collective-permute-start | bytes 1671176 | tf_op jit(solution)/shard_map/ppermute | solution.py:483
  37.7 17.5 %collective-permute-start.5 = (bf16[272,1024]{1,0:T(8,128)(2,1)S(1)}, bf16[272,1024]{1,0:T(8,128)(2,1)S(1)}, u32[]{:S(2)}, u32[]{:S(2)}) collective-permute-start(bf16[272,1024]{1,0:T(8,128)(2,1)S(1)} %collective-permute-done.2.refs_3_.refs_7_.refs_11_), channel_id=1, source_target_pairs={{0,2},{2,0},{4,6},{6,4},{8,10},{10,8},{12,14},{14,12},{16,18},{18,... | collective-permute-start | bytes 1671176 | tf_op jit(solution)/shard_map/ppermute | solution.py:483
  39.2 16.1 %collective-permute-start.7 = (bf16[272,1024]{1,0:T(8,128)(2,1)S(1)}, bf16[272,1024]{1,0:T(8,128)(2,1)S(1)}, u32[]{:S(2)}, u32[]{:S(2)}) collective-permute-start(bf16[272,1024]{1,0:T(8,128)(2,1)S(1)} %collective-permute-done.4), channel_id=1, source_target_pairs={{8,0},{10,2},{12,4},{14,6},{16,24},{18,26},{20,28},{22,30},{9,1},{... | collective-permute-start | bytes 1671176 | tf_op jit(solution)/shard_map/ppermute | solution.py:483
  40.5 1.6 %copy-start.4 = (bf16[256,4096]{1,0:T(8,128)(2,1)S(1)}, bf16[256,4096]{1,0:T(8,128)(2,1)}, u32[]{:S(2)}) copy-start(bf16[256,4096]{1,0:T(8,128)(2,1)} %refs_0_.13) | copy-start | bytes 6291460
  55.3 19.7 %collective-permute-start.12 = (bf16[272,1024]{1,0:T(8,128)(2,1)S(1)}, bf16[272,1024]{1,0:T(8,128)(2,1)S(1)}, u32[]{:S(2)}, u32[]{:S(2)}) collective-permute-start(bf16[272,1024]{1,0:T(8,128)(2,1)S(1)} %collective-permute-done.5.refs_1_.refs_4_.refs_7_), channel_id=1, source_target_pairs={{8,16},{10,18},{12,20},{14,22},{16,8},{18,10},{20,12},{22,14},{9,1... | collective-permute-start | bytes 1671176 | tf_op jit(solution)/shard_map/ppermute | solution.py:483
  56.3 18.7 %collective-permute-start.11 = (bf16[272,1024]{1,0:T(8,128)(2,1)S(1)}, bf16[272,1024]{1,0:T(8,128)(2,1)S(1)}, u32[]{:S(2)}, u32[]{:S(2)}) collective-permute-start(bf16[272,1024]{1,0:T(8,128)(2,1)S(1)} %broadcast_select_fusion.4), channel_id=1, source_target_pairs={{0,8},{2,10},{4,12},{6,14},{8,0},{10,2},{12,4},{14,6},{16,24},{18,... | collective-permute-start | bytes 1671176 | tf_op jit(solution)/shard_map/ppermute | solution.py:483
  61.3 13.8 %collective-permute-start.10 = (bf16[272,1024]{1,0:T(8,128)(2,1)S(1)}, bf16[272,1024]{1,0:T(8,128)(2,1)S(1)}, u32[]{:S(2)}, u32[]{:S(2)}) collective-permute-start(bf16[272,1024]{1,0:T(8,128)(2,1)S(1)} %broadcast_select_fusion.5.refs_3_.refs_6_.refs_9_), channel_id=1, source_target_pairs={{0,4},{2,6},{4,0},{6,2},{8,12},{10,14},{12,8},{14,10},{16,20},{18,... | collective-permute-start | bytes 1671176 | tf_op jit(solution)/shard_map/ppermute | solution.py:483
  62.9 12.2 %collective-permute-start.9 = (bf16[272,1024]{1,0:T(8,128)(2,1)S(1)}, bf16[272,1024]{1,0:T(8,128)(2,1)S(1)}, u32[]{:S(2)}, u32[]{:S(2)}) collective-permute-start(bf16[272,1024]{1,0:T(8,128)(2,1)S(1)} %collective-permute-done.3.refs_4_.refs_8_.refs_12_), channel_id=1, source_target_pairs={{0,2},{2,0},{4,6},{6,4},{8,10},{10,8},{12,14},{14,12},{16,18},{18,... | collective-permute-start | bytes 1671176 | tf_op jit(solution)/shard_map/ppermute | solution.py:483
  75.1 15.9 %collective-permute-start.16 = (bf16[272,1024]{1,0:T(8,128)(2,1)S(1)}, bf16[272,1024]{1,0:T(8,128)(2,1)S(1)}, u32[]{:S(2)}, u32[]{:S(2)}) collective-permute-start(bf16[272,1024]{1,0:T(8,128)(2,1)S(1)} %collective-permute-done.11), channel_id=1, source_target_pairs={{8,16},{10,18},{12,20},{14,22},{16,8},{18,10},{20,12},{22,14},{9,1... | collective-permute-start | bytes 1671176 | tf_op jit(solution)/shard_map/ppermute | solution.py:483
  75.8 15.1 %collective-permute-start.14 = (bf16[272,1024]{1,0:T(8,128)(2,1)S(1)}, bf16[272,1024]{1,0:T(8,128)(2,1)S(1)}, u32[]{:S(2)}, u32[]{:S(2)}) collective-permute-start(bf16[272,1024]{1,0:T(8,128)(2,1)S(1)} %broadcast_select_fusion.3.refs_3_.refs_6_.refs_9_), channel_id=1, source_target_pairs={{0,4},{2,6},{4,0},{6,2},{8,12},{10,14},{12,8},{14,10},{16,20},{18,... | collective-permute-start | bytes 1671176 | tf_op jit(solution)/shard_map/ppermute | solution.py:483
  76.4 14.5 %collective-permute-start.13 = (bf16[272,1024]{1,0:T(8,128)(2,1)S(1)}, bf16[272,1024]{1,0:T(8,128)(2,1)S(1)}, u32[]{:S(2)}, u32[]{:S(2)}) collective-permute-start(bf16[272,1024]{1,0:T(8,128)(2,1)S(1)} %broadcast_select_fusion.5.refs_3_.refs_6_.refs_9_), channel_id=1, source_target_pairs={{0,2},{2,0},{4,6},{6,4},{8,10},{10,8},{12,14},{14,12},{16,18},{18,... | collective-permute-start | bytes 1671176 | tf_op jit(solution)/shard_map/ppermute | solution.py:483
  77.9 13.1 %collective-permute-start.15 = (bf16[272,1024]{1,0:T(8,128)(2,1)S(1)}, bf16[272,1024]{1,0:T(8,128)(2,1)S(1)}, u32[]{:S(2)}, u32[]{:S(2)}) collective-permute-start(bf16[272,1024]{1,0:T(8,128)(2,1)S(1)} %collective-permute-done.12), channel_id=1, source_target_pairs={{8,0},{10,2},{12,4},{14,6},{16,24},{18,26},{20,28},{22,30},{9,1},{... | collective-permute-start | bytes 1671176 | tf_op jit(solution)/shard_map/ppermute | solution.py:483
  91.0 15.3 %collective-permute-start.17 = (bf16[272,1024]{1,0:T(8,128)(2,1)S(1)}, bf16[272,1024]{1,0:T(8,128)(2,1)S(1)}, u32[]{:S(2)}, u32[]{:S(2)}) collective-permute-start(bf16[272,1024]{1,0:T(8,128)(2,1)S(1)} %broadcast_select_fusion.3.refs_3_.refs_6_.refs_9_), channel_id=1, source_target_pairs={{0,2},{2,0},{4,6},{6,4},{8,10},{10,8},{12,14},{14,12},{16,18},{18,... | collective-permute-start | bytes 1671176 | tf_op jit(solution)/shard_map/ppermute | solution.py:483
  91.5 14.7 %collective-permute-start.18 = (bf16[272,1024]{1,0:T(8,128)(2,1)S(1)}, bf16[272,1024]{1,0:T(8,128)(2,1)S(1)}, u32[]{:S(2)}, u32[]{:S(2)}) collective-permute-start(bf16[272,1024]{1,0:T(8,128)(2,1)S(1)} %collective-permute-done.9.refs_1_.refs_4_.refs_7_), channel_id=1, source_target_pairs={{0,4},{2,6},{4,0},{6,2},{8,12},{10,14},{12,8},{14,10},{16,20},{18,... | collective-permute-start | bytes 1671176 | tf_op jit(solution)/shard_map/ppermute | solution.py:483
  93.0 13.2 %collective-permute-start.19 = (bf16[272,1024]{1,0:T(8,128)(2,1)S(1)}, bf16[272,1024]{1,0:T(8,128)(2,1)S(1)}, u32[]{:S(2)}, u32[]{:S(2)}) collective-permute-start(bf16[272,1024]{1,0:T(8,128)(2,1)S(1)} %collective-permute-done.16), channel_id=1, source_target_pairs={{8,0},{10,2},{12,4},{14,6},{16,24},{18,26},{20,28},{22,30},{9,1},{... | collective-permute-start | bytes 1671176 | tf_op jit(solution)/shard_map/ppermute | solution.py:483
  94.6 11.8 %copy-start.1 = (bf16[16,4096]{1,0:T(8,128)(2,1)S(1)}, bf16[16,4096]{1,0:T(8,128)(2,1)}, u32[]{:S(2)}) copy-start(bf16[16,4096]{1,0:T(8,128)(2,1)} %refs_12_.1) | copy-start | bytes 393220
  94.6 11.8 %copy-start.5 = (f32[4,128,128]{2,1,0:T(8,128)S(1)}, f32[4,128,128]{2,1,0:T(8,128)}, u32[]{:S(2)}) copy-start(f32[4,128,128]{2,1,0:T(8,128)} %get-tuple-element.54.refs_13_) | copy-start | bytes 786436
  94.6 11.8 %copy-start.6 = (f32[512,128]{1,0:T(8,128)S(1)}, f32[512,128]{1,0:T(8,128)}, u32[]{:S(2)}) copy-start(f32[512,128]{1,0:T(8,128)} %get-tuple-element.56.refs_15_) | copy-start | bytes 786436
  94.6 11.8 %copy-start.7 = (f32[4,8,128]{2,1,0:T(8,128)S(1)}, f32[4,8,128]{2,1,0:T(8,128)}, u32[]{:S(2)}) copy-start(f32[4,8,128]{2,1,0:T(8,128)} %get-tuple-element.55.refs_14_) | copy-start | bytes 49156
